TPU v7x, 32 devices: a whole 2x2x4 slice. The times are simulated.
32 devices in a mesh: orb: 8 (over y, x, core), band: 4 (over z).
Axes of the slice: x: 2, y: 2, z: 4, core: 2. Of those that a mesh axis runs over, the one named last changes fastest.
Arguments:
- blocks: float32 [192, 32, 64, 64], P('orb'), may hold values from -0.125 to 0.125
- columns: int32 [192, 32], P('orb'), may hold values from 0 to 191, as said below
- counts: int32 [192], P('orb'), may hold values from 8 to 32
- vectors: float32 [12288, 1536], P('orb', 'band'), may hold values from -6 to 6
Outputs:
- filtered: float32 [12288, 1536], P('orb', 'band')
- gram: float32 [1536, 1536], P('band', 'orb')
Inputs may be any that keep to these rules, and one draw needn't show every extreme that they name: `columns`: block column indices of row r lie within 24 block rows of r, counted cyclically modulo 192, are distinct within a row, and slot 0 holds r itself.
All inputs are finite; a program needn't handle non-finite values.
Results may differ from a plain program's by a relative error of at most 0.000088.
Values sent between devices are 32-bit elements; how exact they have to be, the bound alone decides.
No kernel may reach another device: no remote copies, remote signals or barrier semaphores. Data moves between devices by JAX's collectives and lax.ppermute only.
A program may use at most 192 MiB of HBM per device.

v0:
```python
import functools

import jax
import jax.numpy as jnp
from jax import lax
from jax.experimental import pallas as pl
from jax.experimental.pallas import tpu as pltpu
from jax.sharding import PartitionSpec as P

GROUP = 4
LANES = 128
MIB = 1024 * 1024
APPLY_MIB = 10


def split(x):
    hi = x.astype(jnp.bfloat16)
    lo = (x - hi.astype(jnp.float32)).astype(jnp.bfloat16)
    return hi, lo


def densify_kernel(slot_ref, blocks_ref, hi_ref, lo_ref, *, spread, reach):
    blk = blocks_ref.shape[2]
    step = pl.program_id(0)
    tile = (blk, 2 * blk)
    shift = lax.broadcasted_iota(jnp.int32, tile, 1) - lax.broadcasted_iota(jnp.int32, tile, 0)

    def one_row(i, carry):
        row = step * GROUP + i
        start = pl.multiple_of(i * blk, blk)
        for pair in range(spread // 2):
            left = slot_ref[row, 2 * pair]
            right = slot_ref[row, 2 * pair + 1]
            lblk = jnp.where(left >= 0, blocks_ref[i, jnp.maximum(left, 0)], 0.0)
            rblk = jnp.where(right >= 0, blocks_ref[i, jnp.maximum(right, 0)], 0.0)
            both = jnp.concatenate([lblk, rblk], axis=1)
            if reach <= 2 * pair + 1 and 2 * pair < reach + GROUP:
                both = both - jnp.where(shift == (reach + i - 2 * pair) * blk, 0.1, 0.0)
            hi, lo = split(both / 0.9)
            hi_ref[pl.ds(start, blk), pl.ds(pair * 2 * blk, 2 * blk)] = hi
            lo_ref[pl.ds(start, blk), pl.ds(pair * 2 * blk, 2 * blk)] = lo
        return carry

    lax.fori_loop(0, GROUP, one_row, 0)


def densify(slot_of, blocks):
    rows, slots, blk, _ = blocks.shape
    spread = slot_of.shape[1]
    shape = pltpu.VMEM((rows * blk, spread * blk), jnp.bfloat16)
    out = pl.BlockSpec((GROUP * blk, spread * blk), lambda g, _: (g, 0))
    return pl.pallas_call(
        functools.partial(densify_kernel, spread=spread, reach=rows),
        grid_spec=pltpu.PrefetchScalarGridSpec(
            num_scalar_prefetch=1,
            grid=(rows // GROUP,),
            in_specs=[pl.BlockSpec((GROUP, slots, blk, blk), lambda g, _: (g, 0, 0, 0))],
            out_specs=[out, out],
        ),
        out_shape=[shape, shape],
        compiler_params=pltpu.CompilerParams(vmem_limit_bytes=20 * MIB),
        cost_estimate=pl.CostEstimate(flops=0, bytes_accessed=60_000_000, transcendentals=0),
    )(slot_of, blocks)


def apply_kernel(core_ref, hi_ref, lo_ref, near_ref, far_ref, own_ref, *rest, second, turned):
    inside_ref, across_ref = (far_ref, near_ref) if turned else (near_ref, far_ref)
    old_ref = rest[0] if second else None
    out_ref, parts = rest[-2:]
    rows, width = own_ref.shape
    wide = hi_ref.shape[1]
    tall = wide - 2 * rows
    core = core_ref[0]
    for place, ref in ((1, own_ref), (2 - 2 * core, inside_ref), (2 * core, across_ref)):
        there = pl.ds(pl.multiple_of(place * rows, rows), rows)
        parts[there, pl.ds(0, width)], parts[there, pl.ds(width, width)] = split(ref[...])

    def one_group(step, carry):
        start = pl.multiple_of(step * tall, tall)
        here = pl.ds(start, tall)
        reached = pl.ds(start, wide)
        both = jnp.dot(hi_ref[here, :], parts[reached, :], preferred_element_type=jnp.float32)
        other = jnp.dot(
            lo_ref[here, :], parts[reached, pl.ds(0, width)], preferred_element_type=jnp.float32
        )
        product = both[:, :width] + (both[:, width:] + other)
        if second:
            product = 2.0 * product - old_ref[here, :]
        out_ref[here, :] = product
        return carry

    lax.fori_loop(0, rows // tall, one_group, 0)


def apply_step(core, hi, lo, halo, own, old=None, turned=False):
    rows, width = own.shape
    wide = hi.shape[1]
    second = old is not None
    hi, lo = (pltpu.with_memory_space_constraint(x, pltpu.VMEM) for x in (hi, lo))
    vmem = pl.BlockSpec(memory_space=pltpu.VMEM)
    return pl.pallas_call(
        functools.partial(apply_kernel, second=second, turned=turned),
        in_specs=[pl.BlockSpec(memory_space=pltpu.SMEM)] + [vmem] * (6 if second else 5),
        out_specs=vmem,
        out_shape=jax.ShapeDtypeStruct((rows, width), jnp.float32),
        scratch_shapes=[pltpu.VMEM((3 * rows, 2 * width), jnp.bfloat16)],
        compiler_params=pltpu.CompilerParams(vmem_limit_bytes=APPLY_MIB * MIB),
        cost_estimate=pl.CostEstimate(
            flops=8 * rows * wide * width, bytes_accessed=4 * rows * wide, transcendentals=0
        ),
    )(core, hi, lo, *(halo[::-1] if turned else halo), own, *([old] if second else []))


def part_kernel(core_ref, hi_ref, lo_ref, *refs, late):
    out_ref, parts = refs[-2:]
    rows, width = refs[0].shape
    wide = hi_ref.shape[1]
    tall = wide - 2 * rows
    core = core_ref[0]
    places = (core,) if late else (1, 2 - 2 * core)
    for place, ref in zip(places, refs):
        there = pl.ds(pl.multiple_of(place * rows, rows), rows)
        parts[there, pl.ds(0, width)], parts[there, pl.ds(width, width)] = split(ref[...])
    empty = 1 - core if late else 2 * core
    parts[pl.ds(pl.multiple_of(empty * rows, rows), rows), :] = jnp.zeros((rows, 2 * width), jnp.bfloat16)
    size = rows if late else wide - tall
    column = core * (wide - rows) if late else (1 - core) * tall
    shift = core * tall if late else (1 - core) * tall

    def one_group(step, carry):
        here = pl.ds(pl.multiple_of(step * tall, tall), tall)
        reached = pl.ds(pl.multiple_of(step * tall + shift, tall), size)
        columns = pl.ds(pl.multiple_of(column, tall), size)
        both = jnp.dot(hi_ref[here, columns], parts[reached, :], preferred_element_type=jnp.float32)
        other = jnp.dot(
            lo_ref[here, columns], parts[reached, pl.ds(0, width)], preferred_element_type=jnp.float32
        )
        product = both[:, :width] + (both[:, width:] + other)
        if late:
            product = 2.0 * (refs[1][here, :] + product) - refs[2][here, :]
        out_ref[here, :] = product
        return carry

    lax.fori_loop(0, rows // tall, one_group, 0)


def apply_part(core, hi, lo, *ins, late):
    rows, width = ins[0].shape
    hi, lo = (pltpu.with_memory_space_constraint(x, pltpu.VMEM) for x in (hi, lo))
    vmem = pl.BlockSpec(memory_space=pltpu.VMEM)
    return pl.pallas_call(
        functools.partial(part_kernel, late=late),
        in_specs=[pl.BlockSpec(memory_space=pltpu.SMEM)] + [vmem] * (2 + len(ins)),
        out_specs=vmem,
        out_shape=jax.ShapeDtypeStruct((rows, width), jnp.float32),
        scratch_shapes=[pltpu.VMEM(((2 if late else 3) * rows, 2 * width), jnp.bfloat16)],
        compiler_params=pltpu.CompilerParams(vmem_limit_bytes=APPLY_MIB * MIB),
        cost_estimate=pl.CostEstimate(
            flops=(2 if late else 6) * rows * hi.shape[1] * width,
            bytes_accessed=4 * rows * hi.shape[1],
            transcendentals=0,
        ),
    )(core, hi, lo, *ins)


def slot_table(columns, counts):
    rows, slots = columns.shape
    total = rows * lax.axis_size("orb")
    spread = GROUP + 2 * rows
    ids = jnp.arange(rows, dtype=jnp.int32)
    offset = lax.axis_index("orb") * rows - rows
    place = (columns - offset) % total - (ids // GROUP * GROUP)[:, None]
    number = jnp.arange(slots, dtype=jnp.int32)
    place = jnp.where(number[None, :] < counts[:, None], place, -1)
    hit = place[:, :, None] == jnp.arange(spread, dtype=jnp.int32)[None, None, :]
    return jnp.max(jnp.where(hit, number[None, :, None], -1), axis=1)


def neighbours(x):
    size = lax.axis_size("orb")
    inside = [(i, i ^ 1) for i in range(size)]
    across = [(i, (i + 1 if i % 2 else i - 1) % size) for i in range(size)]
    return lax.ppermute(x, "orb", inside), lax.ppermute(x, "orb", across)


def after_that(x, *done):
    return lax.optimization_barrier((x, done))[0]


def store_parts(band_ref, ins, outs):
    hi_ref, lo_ref, thi_ref, tlo_ref = outs
    for place, ref in enumerate(ins):
        x = ref[...]
        width = x.shape[1]
        there = pl.ds(pl.multiple_of(band_ref[place] * width, width), width)
        hi_ref[:, there], lo_ref[:, there] = split(x)
        thi_ref[there, :], tlo_ref[there, :] = split(x.T)


def block_row(target, turned, right, part):
    rows = turned[0][0].shape[0] // 4
    there = pl.ds(pl.multiple_of(target * rows, rows), rows)
    thi = jnp.concatenate([hi[there, :] for hi, lo in turned], axis=0)
    tlo = jnp.concatenate([lo[there, :] for hi, lo in turned], axis=0)
    if part is not None:
        half = thi.shape[0] // 2
        thi, tlo = (x[part * half : (part + 1) * half] for x in (thi, tlo))
    hi_ref, lo_ref = right
    total = jnp.dot(thi, lo_ref[...], preferred_element_type=jnp.float32)
    total += jnp.dot(tlo, hi_ref[...], preferred_element_type=jnp.float32)
    return total + jnp.dot(thi, hi_ref[...], preferred_element_type=jnp.float32)


def rows_of(target_ref, turned, right, outs, plan, old_products=()):
    for place, parts in plan:
        wanted = [part for part, _, _ in parts]
        if old_products:
            total = block_row(target_ref[place], turned, right, None)
            total = jnp.concatenate([old_products[place][...], total], axis=0)
        else:
            total = block_row(target_ref[place], turned, right, wanted[0] if len(wanted) == 1 else None)
        half = total.shape[0] // 2
        for part, out, slot in parts:
            if old_products or len(wanted) == 2:
                outs[out][slot] = total[part * half : (part + 1) * half]
            else:
                outs[out][slot] = total


def chunk_kernel(band_ref, target_ref, *refs, before, upper, plan):
    ins, refs = refs[:4], refs[4:]
    olds, refs = [refs[4 * k : 4 * k + 4] for k in range(before)], refs[4 * before :]
    old_products, refs = (refs[:4], refs[4:]) if upper else ((), refs)
    new, outs = refs[:4], refs[4:]
    store_parts(band_ref, ins, new)
    turned = [x[2:] for x in olds] + [new[2:]]
    if plan is None:
        for place, out in enumerate(outs):
            out[...] = block_row(target_ref[place], turned, new[:2], None)
    else:
        rows_of(target_ref, turned, new[:2], outs, plan, old_products)


def chunk(bands, targets, parts, olds, plan=None, old_products=()):
    rows, width = parts[0].shape
    plain = pltpu.VMEM((rows, 4 * width), jnp.bfloat16)
    turned = pltpu.VMEM((4 * width, rows), jnp.bfloat16)
    high = width * (len(olds) + 1) + (old_products[0].shape[0] if old_products else 0)
    count = 4 if plan is None else 1 + max(out for _, x in plan for _, out, _ in x)
    shape = (high, 4 * width) if plan is None else (2, high // 2, 4 * width)
    product = jax.ShapeDtypeStruct(shape, jnp.float32)
    olds = [pltpu.with_memory_space_constraint(x, pltpu.VMEM) for old in olds for x in old]
    ins = [*parts, *olds, *old_products]
    vmem, smem = pl.BlockSpec(memory_space=pltpu.VMEM), pl.BlockSpec(memory_space=pltpu.SMEM)
    out = pl.pallas_call(
        functools.partial(chunk_kernel, before=len(olds) // 4, upper=bool(old_products), plan=plan),
        in_specs=[smem, smem] + [vmem] * len(ins),
        out_specs=[vmem] * (4 + count),
        out_shape=[plain, plain, turned, turned] + [product] * count,
        compiler_params=pltpu.CompilerParams(vmem_limit_bytes=14 * MIB),
        cost_estimate=pl.CostEstimate(
            flops=96 * high * width * rows, bytes_accessed=8_000_000, transcendentals=0
        ),
    )(bands, targets, *ins)
    return out[:4], list(out[4:])


def product_kernel(target_ref, *refs, plan):
    ins, outs = refs[:-2], refs[-2:]
    rows_of(target_ref, [ins[k : k + 2] for k in range(2, len(ins), 2)], ins[:2], outs, plan)


def product(targets, chunks, plan):
    rows, wide = chunks[-1][0].shape
    ins = [*chunks[-1][:2]] + [x for c in chunks for x in c[2:]]
    ins = [pltpu.with_memory_space_constraint(x, pltpu.VMEM) for x in ins]
    high = wide // 4 * len(chunks)
    vmem = pl.BlockSpec(memory_space=pltpu.VMEM)
    return pl.pallas_call(
        functools.partial(product_kernel, plan=plan),
        in_specs=[pl.BlockSpec(memory_space=pltpu.SMEM)] + [vmem] * len(ins),
        out_specs=[vmem] * 2,
        out_shape=[jax.ShapeDtypeStruct((2, high // 2, wide), jnp.float32)] * 2,
        compiler_params=pltpu.CompilerParams(vmem_limit_bytes=16 * MIB),
        cost_estimate=pl.CostEstimate(
            flops=12 * high * wide * rows, bytes_accessed=4_000_000, transcendentals=0
        ),
    )(targets, *ins)


def middle_kernel(got_a, got_b, ours_a, ours_b, send_a, keep_a, send_b, keep_b):
    for got, ours, send_ref, keep in ((got_a, ours_a, send_a, keep_a), (got_b, ours_b, send_b, keep_b)):
        keep[...] = got[0] + ours[0]
        send_ref[...] = got[1] + ours[1]


def middle(*parts):
    shape = jax.ShapeDtypeStruct(parts[0].shape[1:], jnp.float32)
    vmem = pl.BlockSpec(memory_space=pltpu.VMEM)
    return pl.pallas_call(
        middle_kernel,
        in_specs=[vmem] * 4,
        out_specs=[vmem] * 4,
        out_shape=[shape] * 4,
        compiler_params=pltpu.CompilerParams(vmem_limit_bytes=8 * MIB),
        cost_estimate=pl.CostEstimate(flops=0, bytes_accessed=5_000_000, transcendentals=0),
    )(*parts)


def pick_kernel(goal_ref, *refs):
    ins, outs = refs[:4], refs[4:]
    width = ins[0].shape[1] // 4
    for k, out in enumerate(outs):
        there = pl.ds(pl.multiple_of(goal_ref[k] * width, width), width)
        x, y, u, v = (ref[:, there] for ref in ins)
        total = jnp.concatenate([x + y, u + v], axis=0)
        out[...] = jnp.where(goal_ref[4] > 0, total, 0.0) if k == 3 else total


def pick(goals, parts):
    rows, size = parts[0].shape
    shape = jax.ShapeDtypeStruct((2 * rows, size // 4), jnp.float32)
    vmem = pl.BlockSpec(memory_space=pltpu.VMEM)
    return pl.pallas_call(
        pick_kernel,
        in_specs=[pl.BlockSpec(memory_space=pltpu.SMEM)] + [vmem] * 4,
        out_specs=[vmem] * 4,
        out_shape=[shape] * 4,
        compiler_params=pltpu.CompilerParams(vmem_limit_bytes=8 * MIB),
        cost_estimate=pl.CostEstimate(flops=0, bytes_accessed=3_000_000, transcendentals=0),
    )(goals, *parts)


def assemble_kernel(core_ref, piece_ref, turn_e_ref, turn_l_ref, out_ref, *, scale):
    w = piece_ref.shape[1]
    first = jnp.concatenate([piece_ref[:w, :], turn_e_ref[...].T, turn_l_ref[:w, :].T], axis=0)
    second = jnp.concatenate([piece_ref[w : 3 * w, :], turn_l_ref[w:, :].T], axis=0)
    last = piece_ref[3 * w :, :]
    half = out_ref.shape[0]
    is_first = core_ref[0] == 0
    for k, x in enumerate((first, second, last)):
        out_ref[:, pl.ds(k * w, w)] = jnp.where(is_first, x[:half], x[half:]) * scale


def assemble(core, parts, order):
    w = parts[0].shape[1]
    vmem = pl.BlockSpec(memory_space=pltpu.VMEM)
    return pl.pallas_call(
        functools.partial(assemble_kernel, scale=1.0 / order),
        in_specs=[pl.BlockSpec(memory_space=pltpu.SMEM)] + [vmem] * len(parts),
        out_specs=vmem,
        out_shape=jax.ShapeDtypeStruct((3 * w // 2, 3 * w), jnp.float32),
        compiler_params=pltpu.CompilerParams(vmem_limit_bytes=12 * MIB),
        cost_estimate=pl.CostEstimate(flops=0, bytes_accessed=2_000_000, transcendentals=0),
    )(core, *parts).T


def linear(chip, core, z):
    return (chip * 2 + core) * 4 + z


def send(x, pairs):
    return lax.ppermute(x, ("orb", "band"), pairs)


def mirrored(pairs):
    out = []
    for chip in range(4):
        for a, b in pairs:
            out.append((linear(chip, 0, a), linear(chip, 0, b)))
            out.append((linear(chip, 1, 3 - a), linear(chip, 1, 3 - b)))
    return out


def gather_bands(x):
    return [x] + [send(x, mirrored([(source, 2)])) for source in (0, 1, 3)]


def over_chips(flip):
    return [
        (linear(chip, core, 2 - core), linear(chip ^ flip, core, 2 - core))
        for chip in range(4)
        for core in range(2)
    ]


FLIPS = (3, 1, 2, 0)
FAR = ((0, ((0, 0, 1), (1, 1, 1))), (1, ((1, 1, 0),)), (2, ((0, 0, 0),)))
NEAR = ((1, ((0, 0, 1),)), (2, ((1, 1, 1),)), (3, ((0, 0, 0), (1, 1, 0))))
BOTH = (
    (0, ((0, 0, 1), (1, 1, 1))),
    (1, ((0, 2, 1), (1, 1, 0))),
    (2, ((0, 0, 0), (1, 3, 1))),
    (3, ((0, 2, 0), (1, 3, 0))),
)
EVERY = [(q, c, z) for q in range(4) for c in range(2) for z in range(4)]
SWAP = [(linear(q, c, z), linear(q, 1 - c, z)) for q, c, z in EVERY]
TURN = [(linear(q, c, z), linear(z, c, q)) for q, c, z in EVERY]
TURN_UP = [pair for pair in TURN if pair[0] // 4 % 2 == 1]


def simple_gram(filtered):
    partial_gram = jnp.dot(
        filtered.T,
        lax.all_gather(filtered, "band", axis=1, tiled=True),
        precision=lax.Precision.HIGH,
        preferred_element_type=jnp.float32,
    )
    return lax.psum_scatter(partial_gram, "orb", scatter_dimension=1, tiled=True)


def in_turn(hi, lo, old, order):
    core = (lax.axis_index("orb") & 1)[None]
    first = [apply_step(core, hi, lo, neighbours(x), x) for x in old]
    filtered = [apply_step(core, hi, lo, neighbours(x), x, v) for x, v in zip(first, old)]
    filtered = jnp.concatenate(filtered, axis=1)
    return filtered, simple_gram(filtered) / order


def index_tables():
    orb, z = lax.axis_index("orb"), lax.axis_index("band")
    chip, core = orb >> 1, orb & 1
    bands = jnp.stack([b + core * (3 - 2 * b) for b in (2, 0, 1, 3)])
    holder = (z == 2 - core).astype(jnp.int32)
    goals = jnp.stack([k + core * (3 - 2 * k) for k in (0, 1, 3)] + [z, holder])
    targets = jnp.stack([chip ^ flip for flip in FLIPS])
    return bands, goals, targets, core[None]


def by_symmetry(hi, lo, old, order, tables):
    bands, goals, targets, core = tables

    def one(x, halo, v=None, turned=False):
        return apply_step(core, hi, lo, halo, x, v, turned)

    v0, v1, v2 = old
    hv = [neighbours(x) for x in old]
    f0 = one(v0, hv[0])
    hf0 = neighbours(f0)
    f1 = one(v1, hv[1])
    hf1 = neighbours(f1)
    g0 = one(after_that(f0, f1), hf0, v0)
    z0 = gather_bands(g0)
    f2 = one(after_that(v2, g0), hv[2])
    hf2 = neighbours(f2)
    e1 = apply_part(core, hi, lo, after_that(f1, g0, f2, z0[1]), hf1[0], late=False)
    g1 = apply_part(core, hi, lo, hf1[1], after_that(e1, *z0[1:]), v1, late=True)
    z1 = gather_bands(g1)
    e2 = apply_part(core, hi, lo, after_that(f2, g1), hf2[0], late=False)
    g2 = apply_part(core, hi, lo, hf2[1], e2, v2, late=True)
    z2 = gather_bands(g2)
    c0, upper = chunk(bands, targets, [after_that(z0[0], g2)] + z0[1:], [])
    c1, early = chunk(bands, targets, [after_that(z1[0], upper[0])] + z1[1:], [c0], BOTH, upper)

    def first_step(parts):
        return [send(x, over_chips(flip)) for x, flip in zip(parts, (2, 1))]

    def second_step(got, ours):
        send_a, keep_a, send_b, keep_b = middle(*got, *ours)
        return [keep_a, send(send_a, over_chips(1)), keep_b, send(send_b, over_chips(2))]

    def deliver(parts):
        moved = pick(goals, parts)
        return [moved[3]] + [send(x, mirrored([(2, k)])) for k, x in zip((0, 1, 3), moved)]

    got_e = first_step(early[:2])
    c2, far = chunk(bands, targets, [after_that(z2[0], c1[0])] + z2[1:], [c0, c1], FAR)
    got_l = first_step(far)
    sums_e = second_step([after_that(got_e[0], far[0]), got_e[1]], early[2:])
    near = product(after_that(targets, sums_e[0]), [c0, c1, c2], NEAR)
    sums_l = second_step(got_l, near)
    arrived = [deliver([after_that(sums_e[0], sums_l[0])] + sums_e[1:])]
    sums_l[2] = after_that(sums_l[2], arrived[0][0])
    arrived.append(deliver(sums_l))
    filtered = jnp.concatenate([g0, g1, after_that(g2, near[0])], axis=1)
    piece = jnp.concatenate([(x[0] + x[1]) + (x[2] + x[3]) for x in arrived], axis=0)
    piece = piece + send(piece, SWAP)
    w = v0.shape[1]
    turn_e = send(piece[w : 2 * w], TURN)
    turn_l = send(piece[3 * w : 5 * w], TURN_UP)
    return filtered, assemble(core, [piece, turn_e, turn_l], order)


def body(blocks, columns, counts, vectors, symmetric):
    rows, width = vectors.shape
    order = rows * lax.axis_size("orb")
    slot_of = slot_table(columns, counts)
    later = vectors
    if symmetric:
        tables = index_tables()
        slot_of, tables, later = lax.optimization_barrier((slot_of, tables, vectors))
    old = [
        (later if c else vectors)[:, c : min(c + LANES, width)] for c in range(0, width, LANES)
    ]
    hi, lo = densify(slot_of, blocks)
    if symmetric:
        return by_symmetry(hi, lo, old, order, tables)
    return in_turn(hi, lo, old, order)


def solution(mesh):
    placed = (P("orb", None, None, None), P("orb", None), P("orb"), P("orb", "band"))

    def whole(blocks, columns, counts, vectors):
        symmetric = (
            mesh.shape["orb"] == 8 and mesh.shape["band"] == 4 and vectors.shape[1] == 3 * LANES
        )
        return body(blocks, columns, counts, vectors, symmetric)

    return jax.shard_map(
        whole,
        mesh=mesh,
        in_specs=placed,
        out_specs=(P("orb", "band"), P("band", "orb")),
        check_vma=False,
    )
```

profile of v0, /device:TPU:3, one launch (start us, length us, event | category | flops | bytes accessed | tf_op | source)
XLA Modules:
  0.0 194.9 jit_solution(1304880090087430104)
XLA Ops:
  7.4 12.8 %shard_map.59 = (bf16[1536,3328]{1,0:T(8,128)(2,1)S(1)}, bf16[1536,3328]{1,0:T(8,128)(2,1)S(1)}) custom-call(s32[24,52]{1,0:T(8,128)S(1)} %select_reduce_fusion.slot_ref, f32[24,32,64,64]{3,2,1,0:T(8,128)} %blocks_ref.1), custom_call_target="tpu_custom_call" | custom-call | bytes 60000000 | tf_op jit(solution)/shard_map/pallas_call | solution.py:52
  23.3 6.8 %shard_map.60.own_ref = f32[1536,128]{1,0:T(8,128)S(1)} custom-call(s32[1]{0:T(128)} %bitcast.10.core_ref, bf16[1536,3328]{1,0:T(8,128)(2,1)S(1)} %get-tuple-element.65.hi_ref, bf16[1536,3328]{1,0:T(8,128)(2,1)S(1)} %get-tuple-element.66.lo_ref, f32[1536,128]{1,0:T(8,128)S(1)} %collective-permute-done.near_ref, ...), custom_call_target="tpu_custom_call" | custom-call | flops 5234491392 | bytes 20447232 | tf_op jit(solution)/shard_map/pallas_call | solution.py:101
  33.5 6.6 %collective-permute-done.5.far_ref = f32[1536,128]{1,0:T(8,128)S(1)} collective-permute-done((f32[1536,128]{1,0:T(8,128)S(1)}, f32[1536,128]{1,0:T(8,128)S(1)}, u32[]{:S(2)}, u32[]{:S(2)}) %collective-permute-start.5) | collective-permute-done | bytes 786464 | tf_op jit(solution)/shard_map/ppermute | solution.py:183
  40.1 6.8 %shard_map.61.refs_0_ = f32[1536,128]{1,0:T(8,128)S(1)} custom-call(s32[1]{0:T(128)} %bitcast.10.core_ref, bf16[1536,3328]{1,0:T(8,128)(2,1)S(1)} %get-tuple-element.65.hi_ref, bf16[1536,3328]{1,0:T(8,128)(2,1)S(1)} %get-tuple-element.66.lo_ref, f32[1536,128]{1,0:T(8,128)S(1)} %collective-permute-done.4.near_ref, ...), custom_call_target="tpu_custom_call" | custom-call | flops 5234491392 | bytes 20447232 | tf_op jit(solution)/shard_map/pallas_call | solution.py:101
  46.9 10.0 %collective-permute-done.3.far_ref = f32[1536,128]{1,0:T(8,128)S(1)} collective-permute-done((f32[1536,128]{1,0:T(8,128)S(1)}, f32[1536,128]{1,0:T(8,128)S(1)}, u32[]{:S(2)}, u32[]{:S(2)}) %collective-permute-start.3) | collective-permute-done | bytes 786464 | tf_op jit(solution)/shard_map/ppermute | solution.py:183
  57.0 6.8 %shard_map.62.refs_0_ = f32[1536,128]{1,0:T(8,128)S(1)} custom-call(s32[1]{0:T(128)} %bitcast.10.core_ref, bf16[1536,3328]{1,0:T(8,128)(2,1)S(1)} %get-tuple-element.65.hi_ref, bf16[1536,3328]{1,0:T(8,128)(2,1)S(1)} %get-tuple-element.66.lo_ref, f32[1536,128]{1,0:T(8,128)S(1)} %collective-permute-done.2.near_ref, ...), custom_call_target="tpu_custom_call" | custom-call | flops 5234491392 | bytes 20447232 | tf_op jit(solution)/shard_map/pallas_call | solution.py:101
  66.0 3.7 %collective-permute-start.6 = (f32[1536,128]{1,0:T(8,128)S(1)}, f32[1536,128]{1,0:T(8,128)S(1)}, u32[]{:S(2)}, u32[]{:S(2)}) collective-permute-start(f32[1536,128]{1,0:T(8,128)S(1)} %shard_map.61.refs_0_), channel_id=1, source_target_pairs={{0,28},{4,8},{8,4},{12,16},{16,12},{20,24},{24,20},{28,0},{1,29},{... | collective-permute-start | bytes 2359304 | tf_op jit(solution)/shard_map/ppermute | solution.py:183
  70.5 3.4 %collective-permute-done.8.far_ref = f32[1536,128]{1,0:T(8,128)S(1)} collective-permute-done((f32[1536,128]{1,0:T(8,128)S(1)}, f32[1536,128]{1,0:T(8,128)S(1)}, u32[]{:S(2)}, u32[]{:S(2)}) %collective-permute-start.8) | collective-permute-done | bytes 786464 | tf_op jit(solution)/shard_map/ppermute | solution.py:183
  73.8 3.2 %collective-permute-start.12 = (f32[1536,128]{1,0:T(8,128)S(1)}, f32[1536,128]{1,0:T(8,128)S(1)}, u32[]{:S(2)}, u32[]{:S(2)}) collective-permute-start(f32[1536,128]{1,0:T(8,128)S(1)} %shard_map.62.refs_0_), channel_id=1, source_target_pairs={{3,2},{4,5},{11,10},{12,13},{19,18},{20,21},{27,26},{28,29}} | collective-permute-start | bytes 2359304 | tf_op jit(solution)/shard_map/ppermute | solution.py:363
  77.1 6.8 %shard_map.63.refs_0_ = f32[1536,128]{1,0:T(8,128)S(1)} custom-call(s32[1]{0:T(128)} %bitcast.10.core_ref, bf16[1536,3328]{1,0:T(8,128)(2,1)S(1)} %get-tuple-element.65.hi_ref, bf16[1536,3328]{1,0:T(8,128)(2,1)S(1)} %get-tuple-element.66.lo_ref, f32[1536,128]{1,0:T(8,128)S(1)} %collective-permute-done.7.near_ref, ...), custom_call_target="tpu_custom_call" | custom-call | flops 5234491392 | bytes 20447232 | tf_op jit(solution)/shard_map/pallas_call | solution.py:101
  85.0 6.3 %shard_map.64.refs_1_ = f32[1536,128]{1,0:T(8,128)S(1)} custom-call(s32[1]{0:T(128)} %bitcast.10.core_ref, bf16[1536,3328]{1,0:T(8,128)(2,1)S(1)} %get-tuple-element.65.hi_ref, bf16[1536,3328]{1,0:T(8,128)(2,1)S(1)} %get-tuple-element.66.lo_ref, f32[1536,128]{1,0:T(8,128)S(1)} %shard_map.61.refs_0_, f32[1536,128]{1,0:T(8,128)S(1)} %collective-permute-done.10.refs_1_), custom_call_target="tpu_custom_call" | custom-call | flops 3925868544 | bytes 20447232 | tf_op jit(solution)/shard_map/pallas_call | solution.py:151
  91.4 3.7 %shard_map.65.refs_0_ = f32[1536,128]{1,0:T(8,128)S(1)} custom-call(s32[1]{0:T(128)} %bitcast.10.core_ref, bf16[1536,3328]{1,0:T(8,128)(2,1)S(1)} %get-tuple-element.65.hi_ref, bf16[1536,3328]{1,0:T(8,128)(2,1)S(1)} %get-tuple-element.66.lo_ref, f32[1536,128]{1,0:T(8,128)S(1)} %collective-permute-done.6.refs_0_, f32[1536,128]{1,0:T(8,128)S(1)} %shard_map.64.refs_1_, ...), custom_call_target="tpu_custom_call" | custom-call | flops 1308622848 | bytes 20447232 | tf_op jit(solution)/shard_map/pallas_call | solution.py:151
  96.5 3.9 %collective-permute-start.17 = (f32[1536,128]{1,0:T(8,128)S(1)}, f32[1536,128]{1,0:T(8,128)S(1)}, u32[]{:S(2)}, u32[]{:S(2)}) collective-permute-start(f32[1536,128]{1,0:T(8,128)S(1)} %shard_map.65.refs_0_), channel_id=1, source_target_pairs={{3,2},{4,5},{11,10},{12,13},{19,18},{20,21},{27,26},{28,29}} | collective-permute-start | bytes 2359304 | tf_op jit(solution)/shard_map/ppermute | solution.py:363
  100.4 6.3 %shard_map.66.refs_1_ = f32[1536,128]{1,0:T(8,128)S(1)} custom-call(s32[1]{0:T(128)} %bitcast.10.core_ref, bf16[1536,3328]{1,0:T(8,128)(2,1)S(1)} %get-tuple-element.65.hi_ref, bf16[1536,3328]{1,0:T(8,128)(2,1)S(1)} %get-tuple-element.66.lo_ref, f32[1536,128]{1,0:T(8,128)S(1)} %shard_map.63.refs_0_, f32[1536,128]{1,0:T(8,128)S(1)} %collective-permute-done.14.refs_1_), custom_call_target="tpu_custom_call" | custom-call | flops 3925868544 | bytes 20447232 | tf_op jit(solution)/shard_map/pallas_call | solution.py:151
  107.0 3.7 %shard_map.67.refs_0_ = f32[1536,128]{1,0:T(8,128)S(1)} custom-call(s32[1]{0:T(128)} %bitcast.10.core_ref, bf16[1536,3328]{1,0:T(8,128)(2,1)S(1)} %get-tuple-element.65.hi_ref, bf16[1536,3328]{1,0:T(8,128)(2,1)S(1)} %get-tuple-element.66.lo_ref, f32[1536,128]{1,0:T(8,128)S(1)} %collective-permute-done.13.refs_0_, f32[1536,128]{1,0:T(8,128)S(1)} %shard_map.66.refs_1_, ...), custom_call_target="tpu_custom_call" | custom-call | flops 1308622848 | bytes 20447232 | tf_op jit(solution)/shard_map/pallas_call | solution.py:151
  112.2 6.0 %collective-permute-start.21 = (f32[1536,128]{1,0:T(8,128)S(1)}, f32[1536,128]{1,0:T(8,128)S(1)}, u32[]{:S(2)}, u32[]{:S(2)}) collective-permute-start(f32[1536,128]{1,0:T(8,128)S(1)} %shard_map.67.refs_0_), channel_id=1, source_target_pairs={{3,2},{4,5},{11,10},{12,13},{19,18},{20,21},{27,26},{28,29}} | collective-permute-start | bytes 2359304 | tf_op jit(solution)/shard_map/ppermute | solution.py:363
  118.2 4.4 %shard_map.68 = (bf16[1536,512]{1,0:T(8,128)(2,1)S(1)}, bf16[1536,512]{1,0:T(8,128)(2,1)S(1)}, bf16[512,1536]{1,0:T(8,128)(2,1)S(1)}, bf16[512,1536]{1,0:T(8,128...) custom-call(s32[4]{0:T(128)S(1)} %get-tuple-element.74.band_ref, ...), custom_call_target="tpu_custom_call" | custom-call | flops 2415919104 | bytes 8000000 | tf_op jit(solution)/shard_map/pallas_call | solution.py:255
  122.6 6.8 %shard_map.69 = (bf16[1536,512]{1,0:T(8,128)(2,1)S(1)}, bf16[1536,512]{1,0:T(8,128)(2,1)S(1)}, bf16[512,1536]{1,0:T(8,128)(2,1)S(1)}, bf16[512,1536]{1,0:T(8,128...) custom-call(s32[4]{0:T(128)S(1)} %get-tuple-element.74.band_ref, ...), custom_call_target="tpu_custom_call" | custom-call | flops 7247757312 | bytes 8000000 | tf_op jit(solution)/shard_map/pallas_call | solution.py:255
  131.6 5.5 %shard_map.70 = (bf16[1536,512]{1,0:T(8,128)(2,1)S(1)}, bf16[1536,512]{1,0:T(8,128)(2,1)S(1)}, bf16[512,1536]{1,0:T(8,128)(2,1)S(1)}, bf16[512,1536]{1,0:T(8,128...) custom-call(s32[4]{0:T(128)S(1)} %get-tuple-element.74.band_ref, s32[4]{0:T(128)S(1)} %get-tuple-element.97.target_ref, ...), custom_call_target="tpu_custom_call" | custom-call | flops 7247757312 | bytes 8000000 | tf_op jit(solution)/shard_map/pallas_call | solution.py:255
  140.2 4.4 %shard_map.72 = (f32[2,192,512]{2,1,0:T(8,128)S(1)}, f32[2,192,512]{2,1,0:T(8,128)S(1)}) custom-call(s32[4]{0:T(128)S(1)} %get-tuple-element.97.target_ref, bf16[1536,512]{1,0:T(8,128)(2,1)S(1)} %get-tuple-element.98.refs_0_, bf16[1536,512]{1,0:T(8,128)(2,1)S(1)} %get-tuple-element.99.refs_1_, bf16[512,1536]{1,0:T(8,128)(2,1)S(1)} %get-tuple-element.80.refs_6_.refs_2_, ...), custom_call_target="tpu_custom_call" | custom-call | flops 3623878656 | bytes 4000000 | tf_op jit(solution)/shard_map/pallas_call | solution.py:279
  153.0 18.4 %collective-permute-done.29 = f32[384,128]{1,0:T(8,128)S(1)} collective-permute-done((f32[384,128]{1,0:T(8,128)S(1)}, f32[384,128]{1,0:T(8,128)S(1)}, u32[]{:S(2)}, u32[]{:S(2)}) %collective-permute-start.29) | collective-permute-done | bytes 196640 | tf_op jit(solution)/shard_map/ppermute | solution.py:363
  171.4 4.2 %collective-permute-done.34 = f32[384,128]{1,0:T(8,128)S(1)} collective-permute-done((f32[384,128]{1,0:T(8,128)S(1)}, f32[384,128]{1,0:T(8,128)S(1)}, u32[]{:S(2)}, u32[]{:S(2)}) %collective-permute-start.34) | collective-permute-done | bytes 196640 | tf_op jit(solution)/shard_map/ppermute | solution.py:363
  179.7 5.7 %collective-permute-start.37 = (f32[256,128]{1,0:T(8,128)S(1)}, f32[256,128]{1,0:T(8,128)S(1)}, u32[]{:S(2)}, u32[]{:S(2)}) collective-permute-start(f32[256,128]{1,0:T(8,128)S(1)} %slice.21), channel_id=1, source_target_pairs={{4,4},{5,12},{6,20},{7,28},{12,5},{13,13},{14,21},{15,29},{20,6},{... | collective-permute-start | bytes 393224 | tf_op jit(solution)/shard_map/ppermute | solution.py:363
  188.9 5.2 %collective-permute-done.36.turn_e_ref = f32[128,128]{1,0:T(8,128)S(1)} collective-permute-done((f32[128,128]{1,0:T(8,128)S(1)}, f32[128,128]{1,0:T(8,128)S(1)}, u32[]{:S(2)}, u32[]{:S(2)}) %collective-permute-start.36) | collective-permute-done | bytes 65568 | tf_op jit(solution)/shard_map/ppermute | solution.py:363
  (88 shorter events, 42.2 us)
Async XLA Ops:
  1.8 18.3 %collective-permute-start = (f32[1536,128]{1,0:T(8,128)S(1)}, f32[1536,128]{1,0:T(8,128)S(1)}, u32[]{:S(2)}, u32[]{:S(2)}) collective-permute-start(f32[1536,128]{1,0:T(8,128)S(1)} %slice.15.own_ref.rest_0_), channel_id=1, source_target_pairs={{0,4},{4,0},{8,12},{12,8},{16,20},{20,16},{24,28},{28,24},{1,5},{5... | collective-permute-start | bytes 2359304 | tf_op jit(solution)/shard_map/ppermute | solution.py:183
  2.6 20.7 %collective-permute-start.1 = (f32[1536,128]{1,0:T(8,128)S(1)}, f32[1536,128]{1,0:T(8,128)S(1)}, u32[]{:S(2)}, u32[]{:S(2)}) collective-permute-start(f32[1536,128]{1,0:T(8,128)S(1)} %slice.15.own_ref.rest_0_), channel_id=1, source_target_pairs={{0,28},{4,8},{8,4},{12,16},{16,12},{20,24},{24,20},{28,0},{1,29},{... | collective-permute-start | bytes 2359304 | tf_op jit(solution)/shard_map/ppermute | solution.py:183
  5.7 25.7 %collective-permute-start.4 = (f32[1536,128]{1,0:T(8,128)S(1)}, f32[1536,128]{1,0:T(8,128)S(1)}, u32[]{:S(2)}, u32[]{:S(2)}) collective-permute-start(f32[1536,128]{1,0:T(8,128)S(1)} %get-tuple-element.124.own_ref.refs_2_), channel_id=1, source_target_pairs={{0,4},{4,0},{8,12},{12,8},{16,20},{20,16},{24,28},{28,24},{1,5},{5... | collective-permute-start | bytes 2359304 | tf_op jit(solution)/shard_map/ppermute | solution.py:183
  5.8 34.3 %collective-permute-start.5 = (f32[1536,128]{1,0:T(8,128)S(1)}, f32[1536,128]{1,0:T(8,128)S(1)}, u32[]{:S(2)}, u32[]{:S(2)}) collective-permute-start(f32[1536,128]{1,0:T(8,128)S(1)} %get-tuple-element.124.own_ref.refs_2_), channel_id=1, source_target_pairs={{0,28},{4,8},{8,4},{12,16},{16,12},{20,24},{24,20},{28,0},{1,29},{... | collective-permute-start | bytes 2359304 | tf_op jit(solution)/shard_map/ppermute | solution.py:183
  30.1 16.9 %collective-permute-start.2 = (f32[1536,128]{1,0:T(8,128)S(1)}, f32[1536,128]{1,0:T(8,128)S(1)}, u32[]{:S(2)}, u32[]{:S(2)}) collective-permute-start(f32[1536,128]{1,0:T(8,128)S(1)} %shard_map.60.own_ref), channel_id=1, source_target_pairs={{0,4},{4,0},{8,12},{12,8},{16,20},{20,16},{24,28},{28,24},{1,5},{5... | collective-permute-start | bytes 2359304 | tf_op jit(solution)/shard_map/ppermute | solution.py:183
  30.2 26.8 %collective-permute-start.3 = (f32[1536,128]{1,0:T(8,128)S(1)}, f32[1536,128]{1,0:T(8,128)S(1)}, u32[]{:S(2)}, u32[]{:S(2)}) collective-permute-start(f32[1536,128]{1,0:T(8,128)S(1)} %shard_map.60.own_ref), channel_id=1, source_target_pairs={{0,28},{4,8},{8,4},{12,16},{16,12},{20,24},{24,20},{28,0},{1,29},{... | collective-permute-start | bytes 2359304 | tf_op jit(solution)/shard_map/ppermute | solution.py:183
  31.5 38.3 %collective-permute-start.7 = (f32[1536,128]{1,0:T(8,128)S(1)}, f32[1536,128]{1,0:T(8,128)S(1)}, u32[]{:S(2)}, u32[]{:S(2)}) collective-permute-start(f32[1536,128]{1,0:T(8,128)S(1)} %get-tuple-element.69.own_ref.refs_2_), channel_id=1, source_target_pairs={{0,4},{4,0},{8,12},{12,8},{16,20},{20,16},{24,28},{28,24},{1,5},{5... | collective-permute-start | bytes 2359304 | tf_op jit(solution)/shard_map/ppermute | solution.py:183
  31.5 42.4 %collective-permute-start.8 = (f32[1536,128]{1,0:T(8,128)S(1)}, f32[1536,128]{1,0:T(8,128)S(1)}, u32[]{:S(2)}, u32[]{:S(2)}) collective-permute-start(f32[1536,128]{1,0:T(8,128)S(1)} %get-tuple-element.69.own_ref.refs_2_), channel_id=1, source_target_pairs={{0,28},{4,8},{8,4},{12,16},{16,12},{20,24},{24,20},{28,0},{1,29},{... | collective-permute-start | bytes 2359304 | tf_op jit(solution)/shard_map/ppermute | solution.py:183
  63.8 20.1 %collective-permute-start.9 = (f32[1536,128]{1,0:T(8,128)S(1)}, f32[1536,128]{1,0:T(8,128)S(1)}, u32[]{:S(2)}, u32[]{:S(2)}) collective-permute-start(f32[1536,128]{1,0:T(8,128)S(1)} %shard_map.62.refs_0_), channel_id=1, source_target_pairs={{0,2},{7,5},{8,10},{15,13},{16,18},{23,21},{24,26},{31,29}} | collective-permute-start | bytes 2359304 | tf_op jit(solution)/shard_map/ppermute | solution.py:363
  64.5 19.5 %collective-permute-start.10 = (f32[1536,128]{1,0:T(8,128)S(1)}, f32[1536,128]{1,0:T(8,128)S(1)}, u32[]{:S(2)}, u32[]{:S(2)}) collective-permute-start(f32[1536,128]{1,0:T(8,128)S(1)} %shard_map.61.refs_0_), channel_id=1, source_target_pairs={{0,4},{4,0},{8,12},{12,8},{16,20},{20,16},{24,28},{28,24},{1,5},{5... | collective-permute-start | bytes 2359304 | tf_op jit(solution)/shard_map/ppermute | solution.py:183
  66.0 25.3 %collective-permute-start.6 = (f32[1536,128]{1,0:T(8,128)S(1)}, f32[1536,128]{1,0:T(8,128)S(1)}, u32[]{:S(2)}, u32[]{:S(2)}) collective-permute-start(f32[1536,128]{1,0:T(8,128)S(1)} %shard_map.61.refs_0_), channel_id=1, source_target_pairs={{0,28},{4,8},{8,4},{12,16},{16,12},{20,24},{24,20},{28,0},{1,29},{... | collective-permute-start | bytes 2359304 | tf_op jit(solution)/shard_map/ppermute | solution.py:183
  69.7 21.6 %collective-permute-start.11 = (f32[1536,128]{1,0:T(8,128)S(1)}, f32[1536,128]{1,0:T(8,128)S(1)}, u32[]{:S(2)}, u32[]{:S(2)}) collective-permute-start(f32[1536,128]{1,0:T(8,128)S(1)} %shard_map.62.refs_0_), channel_id=1, source_target_pairs={{1,2},{6,5},{9,10},{14,13},{17,18},{22,21},{25,26},{30,29}} | collective-permute-start | bytes 2359304 | tf_op jit(solution)/shard_map/ppermute | solution.py:363
  73.8 17.5 %collective-permute-start.12 = (f32[1536,128]{1,0:T(8,128)S(1)}, f32[1536,128]{1,0:T(8,128)S(1)}, u32[]{:S(2)}, u32[]{:S(2)}) collective-permute-start(f32[1536,128]{1,0:T(8,128)S(1)} %shard_map.62.refs_0_), channel_id=1, source_target_pairs={{3,2},{4,5},{11,10},{12,13},{19,18},{20,21},{27,26},{28,29}} | collective-permute-start | bytes 2359304 | tf_op jit(solution)/shard_map/ppermute | solution.py:363
  84.0 23.0 %collective-permute-start.13 = (f32[1536,128]{1,0:T(8,128)S(1)}, f32[1536,128]{1,0:T(8,128)S(1)}, u32[]{:S(2)}, u32[]{:S(2)}) collective-permute-start(f32[1536,128]{1,0:T(8,128)S(1)} %shard_map.63.refs_0_), channel_id=1, source_target_pairs={{0,28},{4,8},{8,4},{12,16},{16,12},{20,24},{24,20},{28,0},{1,29},{... | collective-permute-start | bytes 2359304 | tf_op jit(solution)/shard_map/ppermute | solution.py:183
  95.1 17.1 %collective-permute-start.15 = (f32[1536,128]{1,0:T(8,128)S(1)}, f32[1536,128]{1,0:T(8,128)S(1)}, u32[]{:S(2)}, u32[]{:S(2)}) collective-permute-start(f32[1536,128]{1,0:T(8,128)S(1)} %shard_map.65.refs_0_), channel_id=1, source_target_pairs={{0,2},{7,5},{8,10},{15,13},{16,18},{23,21},{24,26},{31,29}} | collective-permute-start | bytes 2359304 | tf_op jit(solution)/shard_map/ppermute | solution.py:363
  95.8 26.8 %collective-permute-start.16 = (f32[1536,128]{1,0:T(8,128)S(1)}, f32[1536,128]{1,0:T(8,128)S(1)}, u32[]{:S(2)}, u32[]{:S(2)}) collective-permute-start(f32[1536,128]{1,0:T(8,128)S(1)} %shard_map.65.refs_0_), channel_id=1, source_target_pairs={{1,2},{6,5},{9,10},{14,13},{17,18},{22,21},{25,26},{30,29}} | collective-permute-start | bytes 2359304 | tf_op jit(solution)/shard_map/ppermute | solution.py:363
  96.5 26.1 %collective-permute-start.17 = (f32[1536,128]{1,0:T(8,128)S(1)}, f32[1536,128]{1,0:T(8,128)S(1)}, u32[]{:S(2)}, u32[]{:S(2)}) collective-permute-start(f32[1536,128]{1,0:T(8,128)S(1)} %shard_map.65.refs_0_), channel_id=1, source_target_pairs={{3,2},{4,5},{11,10},{12,13},{19,18},{20,21},{27,26},{28,29}} | collective-permute-start | bytes 2359304 | tf_op jit(solution)/shard_map/ppermute | solution.py:363
  110.8 20.4 %collective-permute-start.19 = (f32[1536,128]{1,0:T(8,128)S(1)}, f32[1536,128]{1,0:T(8,128)S(1)}, u32[]{:S(2)}, u32[]{:S(2)}) collective-permute-start(f32[1536,128]{1,0:T(8,128)S(1)} %shard_map.67.refs_0_), channel_id=1, source_target_pairs={{0,2},{7,5},{8,10},{15,13},{16,18},{23,21},{24,26},{31,29}} | collective-permute-start | bytes 2359304 | tf_op jit(solution)/shard_map/ppermute | solution.py:363
  111.5 19.7 %collective-permute-start.20 = (f32[1536,128]{1,0:T(8,128)S(1)}, f32[1536,128]{1,0:T(8,128)S(1)}, u32[]{:S(2)}, u32[]{:S(2)}) collective-permute-start(f32[1536,128]{1,0:T(8,128)S(1)} %shard_map.67.refs_0_), channel_id=1, source_target_pairs={{1,2},{6,5},{9,10},{14,13},{17,18},{22,21},{25,26},{30,29}} | collective-permute-start | bytes 2359304 | tf_op jit(solution)/shard_map/ppermute | solution.py:363
  112.2 19.4 %collective-permute-start.21 = (f32[1536,128]{1,0:T(8,128)S(1)}, f32[1536,128]{1,0:T(8,128)S(1)}, u32[]{:S(2)}, u32[]{:S(2)}) collective-permute-start(f32[1536,128]{1,0:T(8,128)S(1)} %shard_map.67.refs_0_), channel_id=1, source_target_pairs={{3,2},{4,5},{11,10},{12,13},{19,18},{20,21},{27,26},{28,29}} | collective-permute-start | bytes 2359304 | tf_op jit(solution)/shard_map/ppermute | solution.py:363
  148.2 23.1 %collective-permute-start.29 = (f32[384,128]{1,0:T(8,128)S(1)}, f32[384,128]{1,0:T(8,128)S(1)}, u32[]{:S(2)}, u32[]{:S(2)}) collective-permute-start(f32[384,128]{1,0:T(8,128)S(1)} %get-tuple-element.115), channel_id=1, source_target_pairs={{2,3},{5,4},{10,11},{13,12},{18,19},{21,20},{26,27},{29,28}} | collective-permute-start | bytes 589832 | tf_op jit(solution)/shard_map/ppermute | solution.py:363
  150.3 21.1 %collective-permute-start.32 = (f32[384,128]{1,0:T(8,128)S(1)}, f32[384,128]{1,0:T(8,128)S(1)}, u32[]{:S(2)}, u32[]{:S(2)}) collective-permute-start(f32[384,128]{1,0:T(8,128)S(1)} %get-tuple-element.121), channel_id=1, source_target_pairs={{2,0},{5,7},{10,8},{13,15},{18,16},{21,23},{26,24},{29,31}} | collective-permute-start | bytes 589832 | tf_op jit(solution)/shard_map/ppermute | solution.py:363
  151.0 20.4 %collective-permute-start.33 = (f32[384,128]{1,0:T(8,128)S(1)}, f32[384,128]{1,0:T(8,128)S(1)}, u32[]{:S(2)}, u32[]{:S(2)}) collective-permute-start(f32[384,128]{1,0:T(8,128)S(1)} %get-tuple-element.122), channel_id=1, source_target_pairs={{2,1},{5,6},{10,9},{13,14},{18,17},{21,22},{26,25},{29,30}} | collective-permute-start | bytes 589832 | tf_op jit(solution)/shard_map/ppermute | solution.py:363
  151.7 23.9 %collective-permute-start.34 = (f32[384,128]{1,0:T(8,128)S(1)}, f32[384,128]{1,0:T(8,128)S(1)}, u32[]{:S(2)}, u32[]{:S(2)}) collective-permute-start(f32[384,128]{1,0:T(8,128)S(1)} %get-tuple-element.123), channel_id=1, source_target_pairs={{2,3},{5,4},{10,11},{13,12},{18,19},{21,20},{26,27},{29,28}} | collective-permute-start | bytes 589832 | tf_op jit(solution)/shard_map/ppermute | solution.py:363
  (16 other events, 114.5 us)
where the time goes:
time: 197 us; the launch traced here: 195 us
  Pallas kernels  83.9 us (43%)
  waiting for transfers between devices  53 us (27%)
  starting transfers between devices  51.9 us (26%)
  local copies, waits for them, and re-layouts  2.8 us (1%)
  other arithmetic  2.08 us (1%)
    ppermute x26, starting transfers between devices, send(): return lax.ppermute(x, ('orb', 'band'), pairs)  38.7 us
    ppermute x26, waiting for transfers between devices, send(): return lax.ppermute(x, ('orb', 'band'), pairs)  29.6 us
    pallas_call x4, Pallas kernels, apply_step(): pl.pallas_call(functools.partial(apply_kernel, second=second, turned=turn...  27.3 us
    ppermute x12, waiting for transfers between devices, neighbours(): return (lax.ppermute(x, 'orb', inside), lax.ppermute(x, 'orb', across))  23.4 us
    pallas_call x4, Pallas kernels, apply_part(): pl.pallas_call(functools.partial(part_kernel, late=late), in_specs=[pl.Bl...  20.1 us
    pallas_call x3, Pallas kernels, chunk(): pl.pallas_call(functools.partial(chunk_kernel, before=len(olds) // 4, upp...  16.7 us
    ppermute x12, starting transfers between devices, neighbours(): return (lax.ppermute(x, 'orb', inside), lax.ppermute(x, 'orb', across))  13.3 us
    pallas_call x1, Pallas kernels, densify(): pl.pallas_call(functools.partial(densify_kernel, spread=spread, reach=row...  12.8 us
  transfers between devices with their start and end apart: 38, of which 10 were waited for; matrix products, arithmetic and copies ran while one was open for 2% of the time, Pallas kernels for 43%

commit v1 on v0

--- a/solution.py
+++ b/solution.py
@@ -372,8 +372,9 @@
     return out
 
 
-def gather_bands(x):
-    return [x] + [send(x, mirrored([(source, 2)])) for source in (0, 1, 3)]
+def gather_bands(x, later=None):
+    last = x if later is None else later
+    return [x] + [send(y, mirrored([(source, 2)])) for source, y in ((0, x), (1, x), (3, last))]
 
 
 def over_chips(flip):
@@ -441,15 +442,15 @@
     hf1 = neighbours(f1)
     g0 = one(after_that(f0, f1), hf0, v0)
     z0 = gather_bands(g0)
-    f2 = one(after_that(v2, g0), hv[2])
+    e1 = apply_part(core, hi, lo, after_that(f1, g0), hf1[0], late=False)
+    f2 = one(after_that(v2, e1), hv[2])
     hf2 = neighbours(f2)
-    e1 = apply_part(core, hi, lo, after_that(f1, g0, f2, z0[1]), hf1[0], late=False)
     g1 = apply_part(core, hi, lo, hf1[1], after_that(e1, *z0[1:]), v1, late=True)
     z1 = gather_bands(g1)
     e2 = apply_part(core, hi, lo, after_that(f2, g1), hf2[0], late=False)
     g2 = apply_part(core, hi, lo, hf2[1], e2, v2, late=True)
-    z2 = gather_bands(g2)
     c0, upper = chunk(bands, targets, [after_that(z0[0], g2)] + z0[1:], [])
+    z2 = gather_bands(g2, after_that(g2, upper[0]))
     c1, early = chunk(bands, targets, [after_that(z1[0], upper[0])] + z1[1:], [c0], BOTH, upper)
 
     def first_step(parts):

time: 197 us -> 197 us (level)
  starting transfers between devices: 51.9 us -> 46.9 us
  waiting for transfers between devices: 53 us -> 58 us
    ppermute x12, starting transfers between devices: 13.3 us -> 9.14 us  [neighbours(): return (lax.ppermute(x, 'orb', inside), lax.ppermute(x, 'orb', across))]
    ppermute x26, waiting for transfers between devices: 29.6 us -> 33.7 us  [send(): return lax.ppermute(x, ('orb', 'band'), pairs)]
  transfers between devices with their start and end apart: 38 -> 38, of which waited for: 10 -> 11; matrix products, arithmetic and copies ran while one was open for 2% -> 2% of each run, Pallas kernels for 43% -> 43%
where the time goes in v1:
time: 197 us; the launch traced here: 195 us
  Pallas kernels  83.9 us (43%)
  waiting for transfers between devices  58 us (29%)
  starting transfers between devices  46.9 us (24%)
  local copies, waits for them, and re-layouts  2.8 us (1%)
  other arithmetic  2.08 us (1%)
    ppermute x26, starting transfers between devices, send(): return lax.ppermute(x, ('orb', 'band'), pairs)  37.8 us
    ppermute x26, waiting for transfers between devices, send(): return lax.ppermute(x, ('orb', 'band'), pairs)  33.7 us
    pallas_call x4, Pallas kernels, apply_step(): pl.pallas_call(functools.partial(apply_kernel, second=second, turned=turn...  27.3 us
    ppermute x12, waiting for transfers between devices, neighbours(): return (lax.ppermute(x, 'orb', inside), lax.ppermute(x, 'orb', across))  24.3 us
    pallas_call x4, Pallas kernels, apply_part(): pl.pallas_call(functools.partial(part_kernel, late=late), in_specs=[pl.Bl...  20.1 us
    pallas_call x3, Pallas kernels, chunk(): pl.pallas_call(functools.partial(chunk_kernel, before=len(olds) // 4, upp...  16.7 us
    pallas_call x1, Pallas kernels, densify(): pl.pallas_call(functools.partial(densify_kernel, spread=spread, reach=row...  12.8 us
    ppermute x12, starting transfers between devices, neighbours(): return (lax.ppermute(x, 'orb', inside), lax.ppermute(x, 'orb', across))  9.14 us
  transfers between devices with their start and end apart: 38, of which 11 were waited for; matrix products, arithmetic and copies ran while one was open for 2% of the time, Pallas kernels for 43%

profile of v1, /device:TPU:3, one launch (start us, length us, event | category | flops | bytes accessed | tf_op | source)
XLA Modules:
  0.0 195.0 jit_solution(3848112751004019140)
XLA Ops:
  7.4 12.8 %shard_map.59 = (bf16[1536,3328]{1,0:T(8,128)(2,1)S(1)}, bf16[1536,3328]{1,0:T(8,128)(2,1)S(1)}) custom-call(s32[24,52]{1,0:T(8,128)S(1)} %select_reduce_fusion.slot_ref, f32[24,32,64,64]{3,2,1,0:T(8,128)} %blocks_ref.1), custom_call_target="tpu_custom_call" | custom-call | bytes 60000000 | tf_op jit(solution)/shard_map/pallas_call | solution.py:52
  23.3 6.8 %shard_map.60.own_ref = f32[1536,128]{1,0:T(8,128)S(1)} custom-call(s32[1]{0:T(128)} %bitcast.10.core_ref, bf16[1536,3328]{1,0:T(8,128)(2,1)S(1)} %get-tuple-element.66.hi_ref, bf16[1536,3328]{1,0:T(8,128)(2,1)S(1)} %get-tuple-element.67.lo_ref, f32[1536,128]{1,0:T(8,128)S(1)} %collective-permute-done.near_ref, ...), custom_call_target="tpu_custom_call" | custom-call | flops 5234491392 | bytes 20447232 | tf_op jit(solution)/shard_map/pallas_call | solution.py:101
  31.5 8.7 %collective-permute-done.5.far_ref = f32[1536,128]{1,0:T(8,128)S(1)} collective-permute-done((f32[1536,128]{1,0:T(8,128)S(1)}, f32[1536,128]{1,0:T(8,128)S(1)}, u32[]{:S(2)}, u32[]{:S(2)}) %collective-permute-start.5) | collective-permute-done | bytes 786464 | tf_op jit(solution)/shard_map/ppermute | solution.py:183
  40.1 6.8 %shard_map.61.refs_0_ = f32[1536,128]{1,0:T(8,128)S(1)} custom-call(s32[1]{0:T(128)} %bitcast.10.core_ref, bf16[1536,3328]{1,0:T(8,128)(2,1)S(1)} %get-tuple-element.66.hi_ref, bf16[1536,3328]{1,0:T(8,128)(2,1)S(1)} %get-tuple-element.67.lo_ref, f32[1536,128]{1,0:T(8,128)S(1)} %collective-permute-done.4.near_ref, ...), custom_call_target="tpu_custom_call" | custom-call | flops 5234491392 | bytes 20447232 | tf_op jit(solution)/shard_map/pallas_call | solution.py:101
  50.2 6.8 %collective-permute-done.3.far_ref = f32[1536,128]{1,0:T(8,128)S(1)} collective-permute-done((f32[1536,128]{1,0:T(8,128)S(1)}, f32[1536,128]{1,0:T(8,128)S(1)}, u32[]{:S(2)}, u32[]{:S(2)}) %collective-permute-start.3) | collective-permute-done | bytes 786464 | tf_op jit(solution)/shard_map/ppermute | solution.py:183
  57.0 6.8 %shard_map.62.refs_0_ = f32[1536,128]{1,0:T(8,128)S(1)} custom-call(s32[1]{0:T(128)} %bitcast.10.core_ref, bf16[1536,3328]{1,0:T(8,128)(2,1)S(1)} %get-tuple-element.66.hi_ref, bf16[1536,3328]{1,0:T(8,128)(2,1)S(1)} %get-tuple-element.67.lo_ref, f32[1536,128]{1,0:T(8,128)S(1)} %collective-permute-done.2.near_ref, ...), custom_call_target="tpu_custom_call" | custom-call | flops 5234491392 | bytes 20447232 | tf_op jit(solution)/shard_map/pallas_call | solution.py:101
  63.8 3.3 %collective-permute-start.10 = (f32[1536,128]{1,0:T(8,128)S(1)}, f32[1536,128]{1,0:T(8,128)S(1)}, u32[]{:S(2)}, u32[]{:S(2)}) collective-permute-start(f32[1536,128]{1,0:T(8,128)S(1)} %shard_map.62.refs_0_), channel_id=1, source_target_pairs={{3,2},{4,5},{11,10},{12,13},{19,18},{20,21},{27,26},{28,29}} | collective-permute-start | bytes 2359304 | tf_op jit(solution)/shard_map/ppermute | solution.py:363
  67.8 6.3 %shard_map.63.refs_1_ = f32[1536,128]{1,0:T(8,128)S(1)} custom-call(s32[1]{0:T(128)} %bitcast.10.core_ref, bf16[1536,3328]{1,0:T(8,128)(2,1)S(1)} %get-tuple-element.66.hi_ref, bf16[1536,3328]{1,0:T(8,128)(2,1)S(1)} %get-tuple-element.67.lo_ref, f32[1536,128]{1,0:T(8,128)S(1)} %shard_map.61.refs_0_, f32[1536,128]{1,0:T(8,128)S(1)} %collective-permute-done.7.refs_1_), custom_call_target="tpu_custom_call" | custom-call | flops 3925868544 | bytes 20447232 | tf_op jit(solution)/shard_map/pallas_call | solution.py:151
  74.9 6.8 %shard_map.65.refs_0_ = f32[1536,128]{1,0:T(8,128)S(1)} custom-call(s32[1]{0:T(128)} %bitcast.10.core_ref, bf16[1536,3328]{1,0:T(8,128)(2,1)S(1)} %get-tuple-element.66.hi_ref, bf16[1536,3328]{1,0:T(8,128)(2,1)S(1)} %get-tuple-element.67.lo_ref, f32[1536,128]{1,0:T(8,128)S(1)} %collective-permute-done.11.near_ref, ...), custom_call_target="tpu_custom_call" | custom-call | flops 5234491392 | bytes 20447232 | tf_op jit(solution)/shard_map/pallas_call | solution.py:101
  85.0 5.7 %collective-permute-done.6.refs_0_ = f32[1536,128]{1,0:T(8,128)S(1)} collective-permute-done((f32[1536,128]{1,0:T(8,128)S(1)}, f32[1536,128]{1,0:T(8,128)S(1)}, u32[]{:S(2)}, u32[]{:S(2)}) %collective-permute-start.6) | collective-permute-done | bytes 786464 | tf_op jit(solution)/shard_map/ppermute | solution.py:183
  90.7 3.7 %shard_map.64.refs_0_ = f32[1536,128]{1,0:T(8,128)S(1)} custom-call(s32[1]{0:T(128)} %bitcast.10.core_ref, bf16[1536,3328]{1,0:T(8,128)(2,1)S(1)} %get-tuple-element.66.hi_ref, bf16[1536,3328]{1,0:T(8,128)(2,1)S(1)} %get-tuple-element.67.lo_ref, f32[1536,128]{1,0:T(8,128)S(1)} %collective-permute-done.6.refs_0_, f32[1536,128]{1,0:T(8,128)S(1)} %shard_map.63.refs_1_, ...), custom_call_target="tpu_custom_call" | custom-call | flops 1308622848 | bytes 20447232 | tf_op jit(solution)/shard_map/pallas_call | solution.py:151
  95.8 4.8 %collective-permute-start.17 = (f32[1536,128]{1,0:T(8,128)S(1)}, f32[1536,128]{1,0:T(8,128)S(1)}, u32[]{:S(2)}, u32[]{:S(2)}) collective-permute-start(f32[1536,128]{1,0:T(8,128)S(1)} %shard_map.64.refs_0_), channel_id=1, source_target_pairs={{3,2},{4,5},{11,10},{12,13},{19,18},{20,21},{27,26},{28,29}} | collective-permute-start | bytes 2359304 | tf_op jit(solution)/shard_map/ppermute | solution.py:363
  100.6 6.3 %shard_map.66.refs_1_ = f32[1536,128]{1,0:T(8,128)S(1)} custom-call(s32[1]{0:T(128)} %bitcast.10.core_ref, bf16[1536,3328]{1,0:T(8,128)(2,1)S(1)} %get-tuple-element.66.hi_ref, bf16[1536,3328]{1,0:T(8,128)(2,1)S(1)} %get-tuple-element.67.lo_ref, f32[1536,128]{1,0:T(8,128)S(1)} %shard_map.65.refs_0_, f32[1536,128]{1,0:T(8,128)S(1)} %collective-permute-done.14.refs_1_), custom_call_target="tpu_custom_call" | custom-call | flops 3925868544 | bytes 20447232 | tf_op jit(solution)/shard_map/pallas_call | solution.py:151
  107.0 3.7 %shard_map.67.refs_0_ = f32[1536,128]{1,0:T(8,128)S(1)} custom-call(s32[1]{0:T(128)} %bitcast.10.core_ref, bf16[1536,3328]{1,0:T(8,128)(2,1)S(1)} %get-tuple-element.66.hi_ref, bf16[1536,3328]{1,0:T(8,128)(2,1)S(1)} %get-tuple-element.67.lo_ref, f32[1536,128]{1,0:T(8,128)S(1)} %collective-permute-done.13.refs_0_, f32[1536,128]{1,0:T(8,128)S(1)} %shard_map.66.refs_1_, ...), custom_call_target="tpu_custom_call" | custom-call | flops 1308622848 | bytes 20447232 | tf_op jit(solution)/shard_map/pallas_call | solution.py:151
  111.5 4.4 %shard_map.68 = (bf16[1536,512]{1,0:T(8,128)(2,1)S(1)}, bf16[1536,512]{1,0:T(8,128)(2,1)S(1)}, bf16[512,1536]{1,0:T(8,128)(2,1)S(1)}, bf16[512,1536]{1,0:T(8,128...) custom-call(s32[4]{0:T(128)S(1)} %get-tuple-element.75.band_ref, ...), custom_call_target="tpu_custom_call" | custom-call | flops 2415919104 | bytes 8000000 | tf_op jit(solution)/shard_map/pallas_call | solution.py:255
  115.9 3.8 %collective-permute-start.21 = (f32[1536,128]{1,0:T(8,128)S(1)}, f32[1536,128]{1,0:T(8,128)S(1)}, u32[]{:S(2)}, u32[]{:S(2)}) collective-permute-start(f32[1536,128]{1,0:T(8,128)S(1)} %shard_map.67.refs_0_), channel_id=1, source_target_pairs={{3,2},{4,5},{11,10},{12,13},{19,18},{20,21},{27,26},{28,29}} | collective-permute-start | bytes 2359304 | tf_op jit(solution)/shard_map/ppermute | solution.py:363
  120.5 6.8 %shard_map.69 = (bf16[1536,512]{1,0:T(8,128)(2,1)S(1)}, bf16[1536,512]{1,0:T(8,128)(2,1)S(1)}, bf16[512,1536]{1,0:T(8,128)(2,1)S(1)}, bf16[512,1536]{1,0:T(8,128...) custom-call(s32[4]{0:T(128)S(1)} %get-tuple-element.75.band_ref, ...), custom_call_target="tpu_custom_call" | custom-call | flops 7247757312 | bytes 8000000 | tf_op jit(solution)/shard_map/pallas_call | solution.py:255
  131.9 5.5 %shard_map.70 = (bf16[1536,512]{1,0:T(8,128)(2,1)S(1)}, bf16[1536,512]{1,0:T(8,128)(2,1)S(1)}, bf16[512,1536]{1,0:T(8,128)(2,1)S(1)}, bf16[512,1536]{1,0:T(8,128...) custom-call(s32[4]{0:T(128)S(1)} %get-tuple-element.75.band_ref, s32[4]{0:T(128)S(1)} %get-tuple-element.99.target_ref, ...), custom_call_target="tpu_custom_call" | custom-call | flops 7247757312 | bytes 8000000 | tf_op jit(solution)/shard_map/pallas_call | solution.py:255
  140.5 4.3 %shard_map.72 = (f32[2,192,512]{2,1,0:T(8,128)S(1)}, f32[2,192,512]{2,1,0:T(8,128)S(1)}) custom-call(s32[4]{0:T(128)S(1)} %get-tuple-element.99.target_ref, bf16[1536,512]{1,0:T(8,128)(2,1)S(1)} %get-tuple-element.100.refs_0_, bf16[1536,512]{1,0:T(8,128)(2,1)S(1)} %get-tuple-element.101.refs_1_, bf16[512,1536]{1,0:T(8,128)(2,1)S(1)} %get-tuple-element.81.refs_6_.refs_2_, ...), custom_call_target="tpu_custom_call" | custom-call | flops 3623878656 | bytes 4000000 | tf_op jit(solution)/shard_map/pallas_call | solution.py:279
  153.3 16.5 %collective-permute-done.29 = f32[384,128]{1,0:T(8,128)S(1)} collective-permute-done((f32[384,128]{1,0:T(8,128)S(1)}, f32[384,128]{1,0:T(8,128)S(1)}, u32[]{:S(2)}, u32[]{:S(2)}) %collective-permute-start.29) | collective-permute-done | bytes 196640 | tf_op jit(solution)/shard_map/ppermute | solution.py:363
  169.9 6.0 %collective-permute-done.34 = f32[384,128]{1,0:T(8,128)S(1)} collective-permute-done((f32[384,128]{1,0:T(8,128)S(1)}, f32[384,128]{1,0:T(8,128)S(1)}, u32[]{:S(2)}, u32[]{:S(2)}) %collective-permute-start.34) | collective-permute-done | bytes 196640 | tf_op jit(solution)/shard_map/ppermute | solution.py:363
  176.0 4.3 %collective-permute-start.35 = (f32[768,128]{1,0:T(8,128)S(1)}, f32[768,128]{1,0:T(8,128)S(1)}, u32[]{:S(2)}, u32[]{:S(2)}) collective-permute-start(f32[768,128]{1,0:T(8,128)S(1)} %pad_maximum_fusion.1), channel_id=1, source_target_pairs={{0,4},{1,5},{2,6},{3,7},{4,0},{5,1},{6,2},{7,3},{8,12},{9,13},{10,... | collective-permute-start | bytes 1179656 | tf_op jit(solution)/shard_map/ppermute | solution.py:363
  181.8 3.7 %collective-permute-start.37 = (f32[256,128]{1,0:T(8,128)S(1)}, f32[256,128]{1,0:T(8,128)S(1)}, u32[]{:S(2)}, u32[]{:S(2)}) collective-permute-start(f32[256,128]{1,0:T(8,128)S(1)} %slice.21), channel_id=1, source_target_pairs={{4,4},{5,12},{6,20},{7,28},{12,5},{13,13},{14,21},{15,29},{20,6},{... | collective-permute-start | bytes 393224 | tf_op jit(solution)/shard_map/ppermute | solution.py:363
  189.5 4.6 %collective-permute-done.36.turn_e_ref = f32[128,128]{1,0:T(8,128)S(1)} collective-permute-done((f32[128,128]{1,0:T(8,128)S(1)}, f32[128,128]{1,0:T(8,128)S(1)}, u32[]{:S(2)}, u32[]{:S(2)}) %collective-permute-start.36) | collective-permute-done | bytes 65568 | tf_op jit(solution)/shard_map/ppermute | solution.py:363
  (88 shorter events, 44.3 us)
Async XLA Ops:
  1.8 18.3 %collective-permute-start = (f32[1536,128]{1,0:T(8,128)S(1)}, f32[1536,128]{1,0:T(8,128)S(1)}, u32[]{:S(2)}, u32[]{:S(2)}) collective-permute-start(f32[1536,128]{1,0:T(8,128)S(1)} %slice.15.own_ref.rest_0_), channel_id=1, source_target_pairs={{0,4},{4,0},{8,12},{12,8},{16,20},{20,16},{24,28},{28,24},{1,5},{5... | collective-permute-start | bytes 2359304 | tf_op jit(solution)/shard_map/ppermute | solution.py:183
  2.6 20.7 %collective-permute-start.1 = (f32[1536,128]{1,0:T(8,128)S(1)}, f32[1536,128]{1,0:T(8,128)S(1)}, u32[]{:S(2)}, u32[]{:S(2)}) collective-permute-start(f32[1536,128]{1,0:T(8,128)S(1)} %slice.15.own_ref.rest_0_), channel_id=1, source_target_pairs={{0,28},{4,8},{8,4},{12,16},{16,12},{20,24},{24,20},{28,0},{1,29},{... | collective-permute-start | bytes 2359304 | tf_op jit(solution)/shard_map/ppermute | solution.py:183
  5.7 25.7 %collective-permute-start.4 = (f32[1536,128]{1,0:T(8,128)S(1)}, f32[1536,128]{1,0:T(8,128)S(1)}, u32[]{:S(2)}, u32[]{:S(2)}) collective-permute-start(f32[1536,128]{1,0:T(8,128)S(1)} %get-tuple-element.126.own_ref.refs_2_), channel_id=1, source_target_pairs={{0,4},{4,0},{8,12},{12,8},{16,20},{20,16},{24,28},{28,24},{1,5},{5... | collective-permute-start | bytes 2359304 | tf_op jit(solution)/shard_map/ppermute | solution.py:183
  5.8 34.3 %collective-permute-start.5 = (f32[1536,128]{1,0:T(8,128)S(1)}, f32[1536,128]{1,0:T(8,128)S(1)}, u32[]{:S(2)}, u32[]{:S(2)}) collective-permute-start(f32[1536,128]{1,0:T(8,128)S(1)} %get-tuple-element.126.own_ref.refs_2_), channel_id=1, source_target_pairs={{0,28},{4,8},{8,4},{12,16},{16,12},{20,24},{24,20},{28,0},{1,29},{... | collective-permute-start | bytes 2359304 | tf_op jit(solution)/shard_map/ppermute | solution.py:183
  30.1 18.7 %collective-permute-start.2 = (f32[1536,128]{1,0:T(8,128)S(1)}, f32[1536,128]{1,0:T(8,128)S(1)}, u32[]{:S(2)}, u32[]{:S(2)}) collective-permute-start(f32[1536,128]{1,0:T(8,128)S(1)} %shard_map.60.own_ref), channel_id=1, source_target_pairs={{0,4},{4,0},{8,12},{12,8},{16,20},{20,16},{24,28},{28,24},{1,5},{5... | collective-permute-start | bytes 2359304 | tf_op jit(solution)/shard_map/ppermute | solution.py:183
  30.2 26.8 %collective-permute-start.3 = (f32[1536,128]{1,0:T(8,128)S(1)}, f32[1536,128]{1,0:T(8,128)S(1)}, u32[]{:S(2)}, u32[]{:S(2)}) collective-permute-start(f32[1536,128]{1,0:T(8,128)S(1)} %shard_map.60.own_ref), channel_id=1, source_target_pairs={{0,28},{4,8},{8,4},{12,16},{16,12},{20,24},{24,20},{28,0},{1,29},{... | collective-permute-start | bytes 2359304 | tf_op jit(solution)/shard_map/ppermute | solution.py:183
  46.9 20.1 %collective-permute-start.7 = (f32[1536,128]{1,0:T(8,128)S(1)}, f32[1536,128]{1,0:T(8,128)S(1)}, u32[]{:S(2)}, u32[]{:S(2)}) collective-permute-start(f32[1536,128]{1,0:T(8,128)S(1)} %shard_map.61.refs_0_), channel_id=1, source_target_pairs={{0,4},{4,0},{8,12},{12,8},{16,20},{20,16},{24,28},{28,24},{1,5},{5... | collective-permute-start | bytes 2359304 | tf_op jit(solution)/shard_map/ppermute | solution.py:183
  47.0 27.1 %collective-permute-start.11 = (f32[1536,128]{1,0:T(8,128)S(1)}, f32[1536,128]{1,0:T(8,128)S(1)}, u32[]{:S(2)}, u32[]{:S(2)}) collective-permute-start(f32[1536,128]{1,0:T(8,128)S(1)} %get-tuple-element.72.own_ref.refs_2_), channel_id=1, source_target_pairs={{0,4},{4,0},{8,12},{12,8},{16,20},{20,16},{24,28},{28,24},{1,5},{5... | collective-permute-start | bytes 2359304 | tf_op jit(solution)/shard_map/ppermute | solution.py:183
  47.5 27.3 %collective-permute-start.12 = (f32[1536,128]{1,0:T(8,128)S(1)}, f32[1536,128]{1,0:T(8,128)S(1)}, u32[]{:S(2)}, u32[]{:S(2)}) collective-permute-start(f32[1536,128]{1,0:T(8,128)S(1)} %get-tuple-element.72.own_ref.refs_2_), channel_id=1, source_target_pairs={{0,28},{4,8},{8,4},{12,16},{16,12},{20,24},{24,20},{28,0},{1,29},{... | collective-permute-start | bytes 2359304 | tf_op jit(solution)/shard_map/ppermute | solution.py:183
  48.7 41.9 %collective-permute-start.6 = (f32[1536,128]{1,0:T(8,128)S(1)}, f32[1536,128]{1,0:T(8,128)S(1)}, u32[]{:S(2)}, u32[]{:S(2)}) collective-permute-start(f32[1536,128]{1,0:T(8,128)S(1)} %shard_map.61.refs_0_), channel_id=1, source_target_pairs={{0,28},{4,8},{8,4},{12,16},{16,12},{20,24},{24,20},{28,0},{1,29},{... | collective-permute-start | bytes 2359304 | tf_op jit(solution)/shard_map/ppermute | solution.py:183
  63.8 20.2 %collective-permute-start.10 = (f32[1536,128]{1,0:T(8,128)S(1)}, f32[1536,128]{1,0:T(8,128)S(1)}, u32[]{:S(2)}, u32[]{:S(2)}) collective-permute-start(f32[1536,128]{1,0:T(8,128)S(1)} %shard_map.62.refs_0_), channel_id=1, source_target_pairs={{3,2},{4,5},{11,10},{12,13},{19,18},{20,21},{27,26},{28,29}} | collective-permute-start | bytes 2359304 | tf_op jit(solution)/shard_map/ppermute | solution.py:363
  67.1 17.9 %collective-permute-start.8 = (f32[1536,128]{1,0:T(8,128)S(1)}, f32[1536,128]{1,0:T(8,128)S(1)}, u32[]{:S(2)}, u32[]{:S(2)}) collective-permute-start(f32[1536,128]{1,0:T(8,128)S(1)} %shard_map.62.refs_0_), channel_id=1, source_target_pairs={{0,2},{7,5},{8,10},{15,13},{16,18},{23,21},{24,26},{31,29}} | collective-permute-start | bytes 2359304 | tf_op jit(solution)/shard_map/ppermute | solution.py:363
  81.7 18.9 %collective-permute-start.14 = (f32[1536,128]{1,0:T(8,128)S(1)}, f32[1536,128]{1,0:T(8,128)S(1)}, u32[]{:S(2)}, u32[]{:S(2)}) collective-permute-start(f32[1536,128]{1,0:T(8,128)S(1)} %shard_map.65.refs_0_), channel_id=1, source_target_pairs={{0,4},{4,0},{8,12},{12,8},{16,20},{20,16},{24,28},{28,24},{1,5},{5... | collective-permute-start | bytes 2359304 | tf_op jit(solution)/shard_map/ppermute | solution.py:183
  84.0 23.0 %collective-permute-start.13 = (f32[1536,128]{1,0:T(8,128)S(1)}, f32[1536,128]{1,0:T(8,128)S(1)}, u32[]{:S(2)}, u32[]{:S(2)}) collective-permute-start(f32[1536,128]{1,0:T(8,128)S(1)} %shard_map.65.refs_0_), channel_id=1, source_target_pairs={{0,28},{4,8},{8,4},{12,16},{16,12},{20,24},{24,20},{28,0},{1,29},{... | collective-permute-start | bytes 2359304 | tf_op jit(solution)/shard_map/ppermute | solution.py:183
  94.4 25.3 %collective-permute-start.15 = (f32[1536,128]{1,0:T(8,128)S(1)}, f32[1536,128]{1,0:T(8,128)S(1)}, u32[]{:S(2)}, u32[]{:S(2)}) collective-permute-start(f32[1536,128]{1,0:T(8,128)S(1)} %shard_map.64.refs_0_), channel_id=1, source_target_pairs={{0,2},{7,5},{8,10},{15,13},{16,18},{23,21},{24,26},{31,29}} | collective-permute-start | bytes 2359304 | tf_op jit(solution)/shard_map/ppermute | solution.py:363
  95.1 25.4 %collective-permute-start.16 = (f32[1536,128]{1,0:T(8,128)S(1)}, f32[1536,128]{1,0:T(8,128)S(1)}, u32[]{:S(2)}, u32[]{:S(2)}) collective-permute-start(f32[1536,128]{1,0:T(8,128)S(1)} %shard_map.64.refs_0_), channel_id=1, source_target_pairs={{1,2},{6,5},{9,10},{14,13},{17,18},{22,21},{25,26},{30,29}} | collective-permute-start | bytes 2359304 | tf_op jit(solution)/shard_map/ppermute | solution.py:363
  95.8 24.6 %collective-permute-start.17 = (f32[1536,128]{1,0:T(8,128)S(1)}, f32[1536,128]{1,0:T(8,128)S(1)}, u32[]{:S(2)}, u32[]{:S(2)}) collective-permute-start(f32[1536,128]{1,0:T(8,128)S(1)} %shard_map.64.refs_0_), channel_id=1, source_target_pairs={{3,2},{4,5},{11,10},{12,13},{19,18},{20,21},{27,26},{28,29}} | collective-permute-start | bytes 2359304 | tf_op jit(solution)/shard_map/ppermute | solution.py:363
  110.8 21.2 %collective-permute-start.19 = (f32[1536,128]{1,0:T(8,128)S(1)}, f32[1536,128]{1,0:T(8,128)S(1)}, u32[]{:S(2)}, u32[]{:S(2)}) collective-permute-start(f32[1536,128]{1,0:T(8,128)S(1)} %shard_map.67.refs_0_), channel_id=1, source_target_pairs={{0,2},{7,5},{8,10},{15,13},{16,18},{23,21},{24,26},{31,29}} | collective-permute-start | bytes 2359304 | tf_op jit(solution)/shard_map/ppermute | solution.py:363
  115.9 16.0 %collective-permute-start.21 = (f32[1536,128]{1,0:T(8,128)S(1)}, f32[1536,128]{1,0:T(8,128)S(1)}, u32[]{:S(2)}, u32[]{:S(2)}) collective-permute-start(f32[1536,128]{1,0:T(8,128)S(1)} %shard_map.67.refs_0_), channel_id=1, source_target_pairs={{3,2},{4,5},{11,10},{12,13},{19,18},{20,21},{27,26},{28,29}} | collective-permute-start | bytes 2359304 | tf_op jit(solution)/shard_map/ppermute | solution.py:363
  148.6 21.3 %collective-permute-start.29 = (f32[384,128]{1,0:T(8,128)S(1)}, f32[384,128]{1,0:T(8,128)S(1)}, u32[]{:S(2)}, u32[]{:S(2)}) collective-permute-start(f32[384,128]{1,0:T(8,128)S(1)} %get-tuple-element.117), channel_id=1, source_target_pairs={{2,3},{5,4},{10,11},{13,12},{18,19},{21,20},{26,27},{29,28}} | collective-permute-start | bytes 589832 | tf_op jit(solution)/shard_map/ppermute | solution.py:363
  150.6 19.3 %collective-permute-start.32 = (f32[384,128]{1,0:T(8,128)S(1)}, f32[384,128]{1,0:T(8,128)S(1)}, u32[]{:S(2)}, u32[]{:S(2)}) collective-permute-start(f32[384,128]{1,0:T(8,128)S(1)} %get-tuple-element.123), channel_id=1, source_target_pairs={{2,0},{5,7},{10,8},{13,15},{18,16},{21,23},{26,24},{29,31}} | collective-permute-start | bytes 589832 | tf_op jit(solution)/shard_map/ppermute | solution.py:363
  151.3 18.6 %collective-permute-start.33 = (f32[384,128]{1,0:T(8,128)S(1)}, f32[384,128]{1,0:T(8,128)S(1)}, u32[]{:S(2)}, u32[]{:S(2)}) collective-permute-start(f32[384,128]{1,0:T(8,128)S(1)} %get-tuple-element.124), channel_id=1, source_target_pairs={{2,1},{5,6},{10,9},{13,14},{18,17},{21,22},{26,25},{29,30}} | collective-permute-start | bytes 589832 | tf_op jit(solution)/shard_map/ppermute | solution.py:363
  152.0 23.9 %collective-permute-start.34 = (f32[384,128]{1,0:T(8,128)S(1)}, f32[384,128]{1,0:T(8,128)S(1)}, u32[]{:S(2)}, u32[]{:S(2)}) collective-permute-start(f32[384,128]{1,0:T(8,128)S(1)} %get-tuple-element.125), channel_id=1, source_target_pairs={{2,3},{5,4},{10,11},{13,12},{18,19},{21,20},{26,27},{29,28}} | collective-permute-start | bytes 589832 | tf_op jit(solution)/shard_map/ppermute | solution.py:363
  181.8 12.3 %collective-permute-start.37 = (f32[256,128]{1,0:T(8,128)S(1)}, f32[256,128]{1,0:T(8,128)S(1)}, u32[]{:S(2)}, u32[]{:S(2)}) collective-permute-start(f32[256,128]{1,0:T(8,128)S(1)} %slice.21), channel_id=1, source_target_pairs={{4,4},{5,12},{6,20},{7,28},{12,5},{13,13},{14,21},{15,29},{20,6},{... | collective-permute-start | bytes 393224 | tf_op jit(solution)/shard_map/ppermute | solution.py:363
  (16 other events, 113.3 us)

commit v2 on v0

--- a/solution.py
+++ b/solution.py
@@ -121,27 +121,40 @@
     for place, ref in zip(places, refs):
         there = pl.ds(pl.multiple_of(place * rows, rows), rows)
         parts[there, pl.ds(0, width)], parts[there, pl.ds(width, width)] = split(ref[...])
-    empty = 1 - core if late else 2 * core
-    parts[pl.ds(pl.multiple_of(empty * rows, rows), rows), :] = jnp.zeros((rows, 2 * width), jnp.bfloat16)
-    size = rows if late else wide - tall
-    column = core * (wide - rows) if late else (1 - core) * tall
-    shift = core * tall if late else (1 - core) * tall
-
-    def one_group(step, carry):
-        here = pl.ds(pl.multiple_of(step * tall, tall), tall)
-        reached = pl.ds(pl.multiple_of(step * tall + shift, tall), size)
-        columns = pl.ds(pl.multiple_of(column, tall), size)
-        both = jnp.dot(hi_ref[here, columns], parts[reached, :], preferred_element_type=jnp.float32)
-        other = jnp.dot(
-            lo_ref[here, columns], parts[reached, pl.ds(0, width)], preferred_element_type=jnp.float32
+    steps = rows // tall
+    half = steps // 2
+    if late:
+        few = (half - 1) * tall
+        empty = pl.ds(pl.multiple_of(rows - core * few, tall), few)
+        runs = (
+            (rows, half * core, core * (wide - rows), core * tall),
+            (half * tall, half * (1 - core), core * (wide - half * tall), core * (half + 1) * tall),
         )
-        product = both[:, :width] + (both[:, width:] + other)
-        if late:
-            product = 2.0 * (refs[1][here, :] + product) - refs[2][here, :]
-        out_ref[here, :] = product
-        return carry
-
-    lax.fori_loop(0, rows // tall, one_group, 0)
+    else:
+        few = rows
+        empty = pl.ds(pl.multiple_of(2 * core * rows, rows), few)
+        runs = ((wide - tall, 0, (1 - core) * tall, (1 - core) * tall),)
+    parts[empty, :] = jnp.zeros((few, 2 * width), jnp.bfloat16)
+    for size, first, column, shift in runs:
+
+        def one_group(k, carry, size=size, first=first, column=column, shift=shift):
+            start = pl.multiple_of((k + first) * tall, tall)
+            here = pl.ds(start, tall)
+            reached = pl.ds(pl.multiple_of(start + shift, tall), size)
+            columns = pl.ds(pl.multiple_of(column, tall), size)
+            both = jnp.dot(hi_ref[here, columns], parts[reached, :], preferred_element_type=jnp.float32)
+            other = jnp.dot(
+                lo_ref[here, columns],
+                parts[reached, pl.ds(0, width)],
+                preferred_element_type=jnp.float32,
+            )
+            product = both[:, :width] + (both[:, width:] + other)
+            if late:
+                product = 2.0 * (refs[1][here, :] + product) - refs[2][here, :]
+            out_ref[here, :] = product
+            return carry
+
+        lax.fori_loop(0, half if late else steps, one_group, 0)
 
 
 def apply_part(core, hi, lo, *ins, late):

time: 197 us -> 196 us (level)
  transfers between devices with their start and end apart: 38 -> 38, of which waited for: 10 -> 10; matrix products, arithmetic and copies ran while one was open for 2% -> 2% of each run, Pallas kernels for 43% -> 42%
where the time goes in v2:
time: 196 us; the launch traced here: 194 us
  Pallas kernels  82.6 us (42%)
  waiting for transfers between devices  53.7 us (27%)
  starting transfers between devices  52 us (27%)
  local copies, waits for them, and re-layouts  2.8 us (1%)
  other arithmetic  2.08 us (1%)
    ppermute x26, starting transfers between devices, send(): return lax.ppermute(x, ('orb', 'band'), pairs)  38.7 us
    ppermute x26, waiting for transfers between devices, send(): return lax.ppermute(x, ('orb', 'band'), pairs)  29.6 us
    pallas_call x4, Pallas kernels, apply_step(): pl.pallas_call(functools.partial(apply_kernel, second=second, turned=turn...  27.3 us
    ppermute x12, waiting for transfers between devices, neighbours(): return (lax.ppermute(x, 'orb', inside), lax.ppermute(x, 'orb', across))  24 us
    pallas_call x4, Pallas kernels, apply_part(): pl.pallas_call(functools.partial(part_kernel, late=late), in_specs=[pl.Bl...  18.7 us
    pallas_call x3, Pallas kernels, chunk(): pl.pallas_call(functools.partial(chunk_kernel, before=len(olds) // 4, upp...  16.7 us
    ppermute x12, starting transfers between devices, neighbours(): return (lax.ppermute(x, 'orb', inside), lax.ppermute(x, 'orb', across))  13.3 us
    pallas_call x1, Pallas kernels, densify(): pl.pallas_call(functools.partial(densify_kernel, spread=spread, reach=row...  12.8 us
  transfers between devices with their start and end apart: 38, of which 10 were waited for; matrix products, arithmetic and copies ran while one was open for 2% of the time, Pallas kernels for 42%

profile of v2, /device:TPU:3, one launch (start us, length us, event | category | flops | bytes accessed | tf_op | source)
XLA Modules:
  0.0 194.3 jit_solution(17788004527706730133)
XLA Ops:
  7.4 12.8 %shard_map.59 = (bf16[1536,3328]{1,0:T(8,128)(2,1)S(1)}, bf16[1536,3328]{1,0:T(8,128)(2,1)S(1)}) custom-call(s32[24,52]{1,0:T(8,128)S(1)} %select_reduce_fusion.slot_ref, f32[24,32,64,64]{3,2,1,0:T(8,128)} %blocks_ref.1), custom_call_target="tpu_custom_call" | custom-call | bytes 60000000 | tf_op jit(solution)/shard_map/pallas_call | solution.py:52
  20.2 3.1 %collective-permute-done.1.far_ref = f32[1536,128]{1,0:T(8,128)S(1)} collective-permute-done((f32[1536,128]{1,0:T(8,128)S(1)}, f32[1536,128]{1,0:T(8,128)S(1)}, u32[]{:S(2)}, u32[]{:S(2)}) %collective-permute-start.1) | collective-permute-done | bytes 786464 | tf_op jit(solution)/shard_map/ppermute | solution.py:196
  23.3 6.8 %shard_map.60.own_ref = f32[1536,128]{1,0:T(8,128)S(1)} custom-call(s32[1]{0:T(128)} %bitcast.10.core_ref, bf16[1536,3328]{1,0:T(8,128)(2,1)S(1)} %get-tuple-element.65.hi_ref, bf16[1536,3328]{1,0:T(8,128)(2,1)S(1)} %get-tuple-element.66.lo_ref, f32[1536,128]{1,0:T(8,128)S(1)} %collective-permute-done.near_ref, ...), custom_call_target="tpu_custom_call" | custom-call | flops 5234491392 | bytes 20447232 | tf_op jit(solution)/shard_map/pallas_call | solution.py:101
  33.5 6.6 %collective-permute-done.5.far_ref = f32[1536,128]{1,0:T(8,128)S(1)} collective-permute-done((f32[1536,128]{1,0:T(8,128)S(1)}, f32[1536,128]{1,0:T(8,128)S(1)}, u32[]{:S(2)}, u32[]{:S(2)}) %collective-permute-start.5) | collective-permute-done | bytes 786464 | tf_op jit(solution)/shard_map/ppermute | solution.py:196
  40.1 6.8 %shard_map.61.refs_0_ = f32[1536,128]{1,0:T(8,128)S(1)} custom-call(s32[1]{0:T(128)} %bitcast.10.core_ref, bf16[1536,3328]{1,0:T(8,128)(2,1)S(1)} %get-tuple-element.65.hi_ref, bf16[1536,3328]{1,0:T(8,128)(2,1)S(1)} %get-tuple-element.66.lo_ref, f32[1536,128]{1,0:T(8,128)S(1)} %collective-permute-done.4.near_ref, ...), custom_call_target="tpu_custom_call" | custom-call | flops 5234491392 | bytes 20447232 | tf_op jit(solution)/shard_map/pallas_call | solution.py:101
  46.9 10.0 %collective-permute-done.3.far_ref = f32[1536,128]{1,0:T(8,128)S(1)} collective-permute-done((f32[1536,128]{1,0:T(8,128)S(1)}, f32[1536,128]{1,0:T(8,128)S(1)}, u32[]{:S(2)}, u32[]{:S(2)}) %collective-permute-start.3) | collective-permute-done | bytes 786464 | tf_op jit(solution)/shard_map/ppermute | solution.py:196
  57.0 6.8 %shard_map.62.refs_0_ = f32[1536,128]{1,0:T(8,128)S(1)} custom-call(s32[1]{0:T(128)} %bitcast.10.core_ref, bf16[1536,3328]{1,0:T(8,128)(2,1)S(1)} %get-tuple-element.65.hi_ref, bf16[1536,3328]{1,0:T(8,128)(2,1)S(1)} %get-tuple-element.66.lo_ref, f32[1536,128]{1,0:T(8,128)S(1)} %collective-permute-done.2.near_ref, ...), custom_call_target="tpu_custom_call" | custom-call | flops 5234491392 | bytes 20447232 | tf_op jit(solution)/shard_map/pallas_call | solution.py:101
  66.0 3.7 %collective-permute-start.6 = (f32[1536,128]{1,0:T(8,128)S(1)}, f32[1536,128]{1,0:T(8,128)S(1)}, u32[]{:S(2)}, u32[]{:S(2)}) collective-permute-start(f32[1536,128]{1,0:T(8,128)S(1)} %shard_map.61.refs_0_), channel_id=1, source_target_pairs={{0,28},{4,8},{8,4},{12,16},{16,12},{20,24},{24,20},{28,0},{1,29},{... | collective-permute-start | bytes 2359304 | tf_op jit(solution)/shard_map/ppermute | solution.py:196
  70.5 3.4 %collective-permute-done.8.far_ref = f32[1536,128]{1,0:T(8,128)S(1)} collective-permute-done((f32[1536,128]{1,0:T(8,128)S(1)}, f32[1536,128]{1,0:T(8,128)S(1)}, u32[]{:S(2)}, u32[]{:S(2)}) %collective-permute-start.8) | collective-permute-done | bytes 786464 | tf_op jit(solution)/shard_map/ppermute | solution.py:196
  73.8 3.2 %collective-permute-start.12 = (f32[1536,128]{1,0:T(8,128)S(1)}, f32[1536,128]{1,0:T(8,128)S(1)}, u32[]{:S(2)}, u32[]{:S(2)}) collective-permute-start(f32[1536,128]{1,0:T(8,128)S(1)} %shard_map.62.refs_0_), channel_id=1, source_target_pairs={{3,2},{4,5},{11,10},{12,13},{19,18},{20,21},{27,26},{28,29}} | collective-permute-start | bytes 2359304 | tf_op jit(solution)/shard_map/ppermute | solution.py:376
  77.1 6.8 %shard_map.63.refs_0_ = f32[1536,128]{1,0:T(8,128)S(1)} custom-call(s32[1]{0:T(128)} %bitcast.10.core_ref, bf16[1536,3328]{1,0:T(8,128)(2,1)S(1)} %get-tuple-element.65.hi_ref, bf16[1536,3328]{1,0:T(8,128)(2,1)S(1)} %get-tuple-element.66.lo_ref, f32[1536,128]{1,0:T(8,128)S(1)} %collective-permute-done.7.near_ref, ...), custom_call_target="tpu_custom_call" | custom-call | flops 5234491392 | bytes 20447232 | tf_op jit(solution)/shard_map/pallas_call | solution.py:101
  85.0 6.3 %shard_map.64.refs_1_ = f32[1536,128]{1,0:T(8,128)S(1)} custom-call(s32[1]{0:T(128)} %bitcast.10.core_ref, bf16[1536,3328]{1,0:T(8,128)(2,1)S(1)} %get-tuple-element.65.hi_ref, bf16[1536,3328]{1,0:T(8,128)(2,1)S(1)} %get-tuple-element.66.lo_ref, f32[1536,128]{1,0:T(8,128)S(1)} %shard_map.61.refs_0_, f32[1536,128]{1,0:T(8,128)S(1)} %collective-permute-done.10.refs_1_), custom_call_target="tpu_custom_call" | custom-call | flops 3925868544 | bytes 20447232 | tf_op jit(solution)/shard_map/pallas_call | solution.py:164
  91.4 3.0 %shard_map.65.refs_0_ = f32[1536,128]{1,0:T(8,128)S(1)} custom-call(s32[1]{0:T(128)} %bitcast.10.core_ref, bf16[1536,3328]{1,0:T(8,128)(2,1)S(1)} %get-tuple-element.65.hi_ref, bf16[1536,3328]{1,0:T(8,128)(2,1)S(1)} %get-tuple-element.66.lo_ref, f32[1536,128]{1,0:T(8,128)S(1)} %collective-permute-done.6.refs_0_, f32[1536,128]{1,0:T(8,128)S(1)} %shard_map.64.refs_1_, ...), custom_call_target="tpu_custom_call" | custom-call | flops 1308622848 | bytes 20447232 | tf_op jit(solution)/shard_map/pallas_call | solution.py:164
  95.8 3.9 %collective-permute-start.17 = (f32[1536,128]{1,0:T(8,128)S(1)}, f32[1536,128]{1,0:T(8,128)S(1)}, u32[]{:S(2)}, u32[]{:S(2)}) collective-permute-start(f32[1536,128]{1,0:T(8,128)S(1)} %shard_map.65.refs_0_), channel_id=1, source_target_pairs={{3,2},{4,5},{11,10},{12,13},{19,18},{20,21},{27,26},{28,29}} | collective-permute-start | bytes 2359304 | tf_op jit(solution)/shard_map/ppermute | solution.py:376
  99.8 6.3 %shard_map.66.refs_1_ = f32[1536,128]{1,0:T(8,128)S(1)} custom-call(s32[1]{0:T(128)} %bitcast.10.core_ref, bf16[1536,3328]{1,0:T(8,128)(2,1)S(1)} %get-tuple-element.65.hi_ref, bf16[1536,3328]{1,0:T(8,128)(2,1)S(1)} %get-tuple-element.66.lo_ref, f32[1536,128]{1,0:T(8,128)S(1)} %shard_map.63.refs_0_, f32[1536,128]{1,0:T(8,128)S(1)} %collective-permute-done.14.refs_1_), custom_call_target="tpu_custom_call" | custom-call | flops 3925868544 | bytes 20447232 | tf_op jit(solution)/shard_map/pallas_call | solution.py:164
  111.5 6.0 %collective-permute-start.21 = (f32[1536,128]{1,0:T(8,128)S(1)}, f32[1536,128]{1,0:T(8,128)S(1)}, u32[]{:S(2)}, u32[]{:S(2)}) collective-permute-start(f32[1536,128]{1,0:T(8,128)S(1)} %shard_map.67.refs_0_), channel_id=1, source_target_pairs={{3,2},{4,5},{11,10},{12,13},{19,18},{20,21},{27,26},{28,29}} | collective-permute-start | bytes 2359304 | tf_op jit(solution)/shard_map/ppermute | solution.py:376
  117.5 4.4 %shard_map.68 = (bf16[1536,512]{1,0:T(8,128)(2,1)S(1)}, bf16[1536,512]{1,0:T(8,128)(2,1)S(1)}, bf16[512,1536]{1,0:T(8,128)(2,1)S(1)}, bf16[512,1536]{1,0:T(8,128...) custom-call(s32[4]{0:T(128)S(1)} %get-tuple-element.74.band_ref, ...), custom_call_target="tpu_custom_call" | custom-call | flops 2415919104 | bytes 8000000 | tf_op jit(solution)/shard_map/pallas_call | solution.py:268
  121.9 6.8 %shard_map.69 = (bf16[1536,512]{1,0:T(8,128)(2,1)S(1)}, bf16[1536,512]{1,0:T(8,128)(2,1)S(1)}, bf16[512,1536]{1,0:T(8,128)(2,1)S(1)}, bf16[512,1536]{1,0:T(8,128...) custom-call(s32[4]{0:T(128)S(1)} %get-tuple-element.74.band_ref, ...), custom_call_target="tpu_custom_call" | custom-call | flops 7247757312 | bytes 8000000 | tf_op jit(solution)/shard_map/pallas_call | solution.py:268
  131.0 5.5 %shard_map.70 = (bf16[1536,512]{1,0:T(8,128)(2,1)S(1)}, bf16[1536,512]{1,0:T(8,128)(2,1)S(1)}, bf16[512,1536]{1,0:T(8,128)(2,1)S(1)}, bf16[512,1536]{1,0:T(8,128...) custom-call(s32[4]{0:T(128)S(1)} %get-tuple-element.74.band_ref, s32[4]{0:T(128)S(1)} %get-tuple-element.97.target_ref, ...), custom_call_target="tpu_custom_call" | custom-call | flops 7247757312 | bytes 8000000 | tf_op jit(solution)/shard_map/pallas_call | solution.py:268
  139.5 4.4 %shard_map.72 = (f32[2,192,512]{2,1,0:T(8,128)S(1)}, f32[2,192,512]{2,1,0:T(8,128)S(1)}) custom-call(s32[4]{0:T(128)S(1)} %get-tuple-element.97.target_ref, bf16[1536,512]{1,0:T(8,128)(2,1)S(1)} %get-tuple-element.98.refs_0_, bf16[1536,512]{1,0:T(8,128)(2,1)S(1)} %get-tuple-element.99.refs_1_, bf16[512,1536]{1,0:T(8,128)(2,1)S(1)} %get-tuple-element.80.refs_6_.refs_2_, ...), custom_call_target="tpu_custom_call" | custom-call | flops 3623878656 | bytes 4000000 | tf_op jit(solution)/shard_map/pallas_call | solution.py:292
  152.3 18.3 %collective-permute-done.29 = f32[384,128]{1,0:T(8,128)S(1)} collective-permute-done((f32[384,128]{1,0:T(8,128)S(1)}, f32[384,128]{1,0:T(8,128)S(1)}, u32[]{:S(2)}, u32[]{:S(2)}) %collective-permute-start.29) | collective-permute-done | bytes 196640 | tf_op jit(solution)/shard_map/ppermute | solution.py:376
  170.8 4.2 %collective-permute-done.34 = f32[384,128]{1,0:T(8,128)S(1)} collective-permute-done((f32[384,128]{1,0:T(8,128)S(1)}, f32[384,128]{1,0:T(8,128)S(1)}, u32[]{:S(2)}, u32[]{:S(2)}) %collective-permute-start.34) | collective-permute-done | bytes 196640 | tf_op jit(solution)/shard_map/ppermute | solution.py:376
  179.1 5.7 %collective-permute-start.37 = (f32[256,128]{1,0:T(8,128)S(1)}, f32[256,128]{1,0:T(8,128)S(1)}, u32[]{:S(2)}, u32[]{:S(2)}) collective-permute-start(f32[256,128]{1,0:T(8,128)S(1)} %slice.21), channel_id=1, source_target_pairs={{4,4},{5,12},{6,20},{7,28},{12,5},{13,13},{14,21},{15,29},{20,6},{... | collective-permute-start | bytes 393224 | tf_op jit(solution)/shard_map/ppermute | solution.py:376
  188.3 5.2 %collective-permute-done.36.turn_e_ref = f32[128,128]{1,0:T(8,128)S(1)} collective-permute-done((f32[128,128]{1,0:T(8,128)S(1)}, f32[128,128]{1,0:T(8,128)S(1)}, u32[]{:S(2)}, u32[]{:S(2)}) %collective-permute-start.36) | collective-permute-done | bytes 65568 | tf_op jit(solution)/shard_map/ppermute | solution.py:376
  (88 shorter events, 42.9 us)
Async XLA Ops:
  1.8 18.3 %collective-permute-start = (f32[1536,128]{1,0:T(8,128)S(1)}, f32[1536,128]{1,0:T(8,128)S(1)}, u32[]{:S(2)}, u32[]{:S(2)}) collective-permute-start(f32[1536,128]{1,0:T(8,128)S(1)} %slice.15.own_ref.rest_0_), channel_id=1, source_target_pairs={{0,4},{4,0},{8,12},{12,8},{16,20},{20,16},{24,28},{28,24},{1,5},{5... | collective-permute-start | bytes 2359304 | tf_op jit(solution)/shard_map/ppermute | solution.py:196
  2.6 20.7 %collective-permute-start.1 = (f32[1536,128]{1,0:T(8,128)S(1)}, f32[1536,128]{1,0:T(8,128)S(1)}, u32[]{:S(2)}, u32[]{:S(2)}) collective-permute-start(f32[1536,128]{1,0:T(8,128)S(1)} %slice.15.own_ref.rest_0_), channel_id=1, source_target_pairs={{0,28},{4,8},{8,4},{12,16},{16,12},{20,24},{24,20},{28,0},{1,29},{... | collective-permute-start | bytes 2359304 | tf_op jit(solution)/shard_map/ppermute | solution.py:196
  5.7 25.7 %collective-permute-start.4 = (f32[1536,128]{1,0:T(8,128)S(1)}, f32[1536,128]{1,0:T(8,128)S(1)}, u32[]{:S(2)}, u32[]{:S(2)}) collective-permute-start(f32[1536,128]{1,0:T(8,128)S(1)} %get-tuple-element.124.own_ref.refs_2_), channel_id=1, source_target_pairs={{0,4},{4,0},{8,12},{12,8},{16,20},{20,16},{24,28},{28,24},{1,5},{5... | collective-permute-start | bytes 2359304 | tf_op jit(solution)/shard_map/ppermute | solution.py:196
  5.8 34.3 %collective-permute-start.5 = (f32[1536,128]{1,0:T(8,128)S(1)}, f32[1536,128]{1,0:T(8,128)S(1)}, u32[]{:S(2)}, u32[]{:S(2)}) collective-permute-start(f32[1536,128]{1,0:T(8,128)S(1)} %get-tuple-element.124.own_ref.refs_2_), channel_id=1, source_target_pairs={{0,28},{4,8},{8,4},{12,16},{16,12},{20,24},{24,20},{28,0},{1,29},{... | collective-permute-start | bytes 2359304 | tf_op jit(solution)/shard_map/ppermute | solution.py:196
  30.1 16.9 %collective-permute-start.2 = (f32[1536,128]{1,0:T(8,128)S(1)}, f32[1536,128]{1,0:T(8,128)S(1)}, u32[]{:S(2)}, u32[]{:S(2)}) collective-permute-start(f32[1536,128]{1,0:T(8,128)S(1)} %shard_map.60.own_ref), channel_id=1, source_target_pairs={{0,4},{4,0},{8,12},{12,8},{16,20},{20,16},{24,28},{28,24},{1,5},{5... | collective-permute-start | bytes 2359304 | tf_op jit(solution)/shard_map/ppermute | solution.py:196
  30.2 26.8 %collective-permute-start.3 = (f32[1536,128]{1,0:T(8,128)S(1)}, f32[1536,128]{1,0:T(8,128)S(1)}, u32[]{:S(2)}, u32[]{:S(2)}) collective-permute-start(f32[1536,128]{1,0:T(8,128)S(1)} %shard_map.60.own_ref), channel_id=1, source_target_pairs={{0,28},{4,8},{8,4},{12,16},{16,12},{20,24},{24,20},{28,0},{1,29},{... | collective-permute-start | bytes 2359304 | tf_op jit(solution)/shard_map/ppermute | solution.py:196
  31.5 38.3 %collective-permute-start.7 = (f32[1536,128]{1,0:T(8,128)S(1)}, f32[1536,128]{1,0:T(8,128)S(1)}, u32[]{:S(2)}, u32[]{:S(2)}) collective-permute-start(f32[1536,128]{1,0:T(8,128)S(1)} %get-tuple-element.69.own_ref.refs_2_), channel_id=1, source_target_pairs={{0,4},{4,0},{8,12},{12,8},{16,20},{20,16},{24,28},{28,24},{1,5},{5... | collective-permute-start | bytes 2359304 | tf_op jit(solution)/shard_map/ppermute | solution.py:196
  31.5 42.4 %collective-permute-start.8 = (f32[1536,128]{1,0:T(8,128)S(1)}, f32[1536,128]{1,0:T(8,128)S(1)}, u32[]{:S(2)}, u32[]{:S(2)}) collective-permute-start(f32[1536,128]{1,0:T(8,128)S(1)} %get-tuple-element.69.own_ref.refs_2_), channel_id=1, source_target_pairs={{0,28},{4,8},{8,4},{12,16},{16,12},{20,24},{24,20},{28,0},{1,29},{... | collective-permute-start | bytes 2359304 | tf_op jit(solution)/shard_map/ppermute | solution.py:196
  63.8 20.1 %collective-permute-start.9 = (f32[1536,128]{1,0:T(8,128)S(1)}, f32[1536,128]{1,0:T(8,128)S(1)}, u32[]{:S(2)}, u32[]{:S(2)}) collective-permute-start(f32[1536,128]{1,0:T(8,128)S(1)} %shard_map.62.refs_0_), channel_id=1, source_target_pairs={{0,2},{7,5},{8,10},{15,13},{16,18},{23,21},{24,26},{31,29}} | collective-permute-start | bytes 2359304 | tf_op jit(solution)/shard_map/ppermute | solution.py:376
  64.5 19.5 %collective-permute-start.10 = (f32[1536,128]{1,0:T(8,128)S(1)}, f32[1536,128]{1,0:T(8,128)S(1)}, u32[]{:S(2)}, u32[]{:S(2)}) collective-permute-start(f32[1536,128]{1,0:T(8,128)S(1)} %shard_map.61.refs_0_), channel_id=1, source_target_pairs={{0,4},{4,0},{8,12},{12,8},{16,20},{20,16},{24,28},{28,24},{1,5},{5... | collective-permute-start | bytes 2359304 | tf_op jit(solution)/shard_map/ppermute | solution.py:196
  66.0 25.3 %collective-permute-start.6 = (f32[1536,128]{1,0:T(8,128)S(1)}, f32[1536,128]{1,0:T(8,128)S(1)}, u32[]{:S(2)}, u32[]{:S(2)}) collective-permute-start(f32[1536,128]{1,0:T(8,128)S(1)} %shard_map.61.refs_0_), channel_id=1, source_target_pairs={{0,28},{4,8},{8,4},{12,16},{16,12},{20,24},{24,20},{28,0},{1,29},{... | collective-permute-start | bytes 2359304 | tf_op jit(solution)/shard_map/ppermute | solution.py:196
  69.7 21.6 %collective-permute-start.11 = (f32[1536,128]{1,0:T(8,128)S(1)}, f32[1536,128]{1,0:T(8,128)S(1)}, u32[]{:S(2)}, u32[]{:S(2)}) collective-permute-start(f32[1536,128]{1,0:T(8,128)S(1)} %shard_map.62.refs_0_), channel_id=1, source_target_pairs={{1,2},{6,5},{9,10},{14,13},{17,18},{22,21},{25,26},{30,29}} | collective-permute-start | bytes 2359304 | tf_op jit(solution)/shard_map/ppermute | solution.py:376
  73.8 17.5 %collective-permute-start.12 = (f32[1536,128]{1,0:T(8,128)S(1)}, f32[1536,128]{1,0:T(8,128)S(1)}, u32[]{:S(2)}, u32[]{:S(2)}) collective-permute-start(f32[1536,128]{1,0:T(8,128)S(1)} %shard_map.62.refs_0_), channel_id=1, source_target_pairs={{3,2},{4,5},{11,10},{12,13},{19,18},{20,21},{27,26},{28,29}} | collective-permute-start | bytes 2359304 | tf_op jit(solution)/shard_map/ppermute | solution.py:376
  84.0 23.0 %collective-permute-start.13 = (f32[1536,128]{1,0:T(8,128)S(1)}, f32[1536,128]{1,0:T(8,128)S(1)}, u32[]{:S(2)}, u32[]{:S(2)}) collective-permute-start(f32[1536,128]{1,0:T(8,128)S(1)} %shard_map.63.refs_0_), channel_id=1, source_target_pairs={{0,28},{4,8},{8,4},{12,16},{16,12},{20,24},{24,20},{28,0},{1,29},{... | collective-permute-start | bytes 2359304 | tf_op jit(solution)/shard_map/ppermute | solution.py:196
  94.4 17.1 %collective-permute-start.15 = (f32[1536,128]{1,0:T(8,128)S(1)}, f32[1536,128]{1,0:T(8,128)S(1)}, u32[]{:S(2)}, u32[]{:S(2)}) collective-permute-start(f32[1536,128]{1,0:T(8,128)S(1)} %shard_map.65.refs_0_), channel_id=1, source_target_pairs={{0,2},{7,5},{8,10},{15,13},{16,18},{23,21},{24,26},{31,29}} | collective-permute-start | bytes 2359304 | tf_op jit(solution)/shard_map/ppermute | solution.py:376
  95.1 26.8 %collective-permute-start.16 = (f32[1536,128]{1,0:T(8,128)S(1)}, f32[1536,128]{1,0:T(8,128)S(1)}, u32[]{:S(2)}, u32[]{:S(2)}) collective-permute-start(f32[1536,128]{1,0:T(8,128)S(1)} %shard_map.65.refs_0_), channel_id=1, source_target_pairs={{1,2},{6,5},{9,10},{14,13},{17,18},{22,21},{25,26},{30,29}} | collective-permute-start | bytes 2359304 | tf_op jit(solution)/shard_map/ppermute | solution.py:376
  95.8 26.1 %collective-permute-start.17 = (f32[1536,128]{1,0:T(8,128)S(1)}, f32[1536,128]{1,0:T(8,128)S(1)}, u32[]{:S(2)}, u32[]{:S(2)}) collective-permute-start(f32[1536,128]{1,0:T(8,128)S(1)} %shard_map.65.refs_0_), channel_id=1, source_target_pairs={{3,2},{4,5},{11,10},{12,13},{19,18},{20,21},{27,26},{28,29}} | collective-permute-start | bytes 2359304 | tf_op jit(solution)/shard_map/ppermute | solution.py:376
  110.1 20.3 %collective-permute-start.19 = (f32[1536,128]{1,0:T(8,128)S(1)}, f32[1536,128]{1,0:T(8,128)S(1)}, u32[]{:S(2)}, u32[]{:S(2)}) collective-permute-start(f32[1536,128]{1,0:T(8,128)S(1)} %shard_map.67.refs_0_), channel_id=1, source_target_pairs={{0,2},{7,5},{8,10},{15,13},{16,18},{23,21},{24,26},{31,29}} | collective-permute-start | bytes 2359304 | tf_op jit(solution)/shard_map/ppermute | solution.py:376
  110.8 19.6 %collective-permute-start.20 = (f32[1536,128]{1,0:T(8,128)S(1)}, f32[1536,128]{1,0:T(8,128)S(1)}, u32[]{:S(2)}, u32[]{:S(2)}) collective-permute-start(f32[1536,128]{1,0:T(8,128)S(1)} %shard_map.67.refs_0_), channel_id=1, source_target_pairs={{1,2},{6,5},{9,10},{14,13},{17,18},{22,21},{25,26},{30,29}} | collective-permute-start | bytes 2359304 | tf_op jit(solution)/shard_map/ppermute | solution.py:376
  111.5 19.4 %collective-permute-start.21 = (f32[1536,128]{1,0:T(8,128)S(1)}, f32[1536,128]{1,0:T(8,128)S(1)}, u32[]{:S(2)}, u32[]{:S(2)}) collective-permute-start(f32[1536,128]{1,0:T(8,128)S(1)} %shard_map.67.refs_0_), channel_id=1, source_target_pairs={{3,2},{4,5},{11,10},{12,13},{19,18},{20,21},{27,26},{28,29}} | collective-permute-start | bytes 2359304 | tf_op jit(solution)/shard_map/ppermute | solution.py:376
  147.6 23.1 %collective-permute-start.29 = (f32[384,128]{1,0:T(8,128)S(1)}, f32[384,128]{1,0:T(8,128)S(1)}, u32[]{:S(2)}, u32[]{:S(2)}) collective-permute-start(f32[384,128]{1,0:T(8,128)S(1)} %get-tuple-element.115), channel_id=1, source_target_pairs={{2,3},{5,4},{10,11},{13,12},{18,19},{21,20},{26,27},{29,28}} | collective-permute-start | bytes 589832 | tf_op jit(solution)/shard_map/ppermute | solution.py:376
  149.7 21.1 %collective-permute-start.32 = (f32[384,128]{1,0:T(8,128)S(1)}, f32[384,128]{1,0:T(8,128)S(1)}, u32[]{:S(2)}, u32[]{:S(2)}) collective-permute-start(f32[384,128]{1,0:T(8,128)S(1)} %get-tuple-element.121), channel_id=1, source_target_pairs={{2,0},{5,7},{10,8},{13,15},{18,16},{21,23},{26,24},{29,31}} | collective-permute-start | bytes 589832 | tf_op jit(solution)/shard_map/ppermute | solution.py:376
  150.3 20.4 %collective-permute-start.33 = (f32[384,128]{1,0:T(8,128)S(1)}, f32[384,128]{1,0:T(8,128)S(1)}, u32[]{:S(2)}, u32[]{:S(2)}) collective-permute-start(f32[384,128]{1,0:T(8,128)S(1)} %get-tuple-element.122), channel_id=1, source_target_pairs={{2,1},{5,6},{10,9},{13,14},{18,17},{21,22},{26,25},{29,30}} | collective-permute-start | bytes 589832 | tf_op jit(solution)/shard_map/ppermute | solution.py:376
  151.0 23.9 %collective-permute-start.34 = (f32[384,128]{1,0:T(8,128)S(1)}, f32[384,128]{1,0:T(8,128)S(1)}, u32[]{:S(2)}, u32[]{:S(2)}) collective-permute-start(f32[384,128]{1,0:T(8,128)S(1)} %get-tuple-element.123), channel_id=1, source_target_pairs={{2,3},{5,4},{10,11},{13,12},{18,19},{21,20},{26,27},{29,28}} | collective-permute-start | bytes 589832 | tf_op jit(solution)/shard_map/ppermute | solution.py:376
  (16 other events, 114.0 us)
